TPU v7x, 128 devices: a whole 4x4x4 slice. The times are simulated.
128 devices in a mesh: tile: 8 (over x, core), scan: 16 (over y, z).
Axes of the slice: x: 4, y: 4, z: 4, core: 2. Of those that a mesh axis runs over, the one named last changes fastest.
Arguments:
- specimen: float32 [2, 2048, 4096], P(None, 'tile', 'scan'), may hold values from -6 to 6
- sampler_noise: float32 [2, 2048, 4096], P(None, 'tile', 'scan'), may hold values from -6 to 6
- probe_field: float32 [2, 256, 256], replicated, may hold values from -6 to 6
- amplitudes: bfloat16 [8, 16, 16, 2, 256, 256], P('tile', 'scan'), may hold values from 0.5 to 4
- corner_rows: int32 [8, 16, 16, 2], P('tile', 'scan'), may hold values from 0 to 256
- corner_cols: int32 [8, 16, 16, 2], P('tile', 'scan'), may hold values from 0 to 256
- slot_counts: int32 [8, 16, 16], P('tile', 'scan'), may hold values from 0 to 2, as said below
- first_weight: bfloat16 [128, 18], replicated, may hold values from -1.5 to 1.5
- first_bias: float32 [128], replicated, may hold values from -3 to 3
- second_weight: bfloat16 [18, 128], replicated, may hold values from -0.1875 to 0.1875
- second_bias: float32 [2], replicated, may hold values from -3 to 3
Outputs:
- updated: float32 [2, 2048, 4096], P(None, 'tile', 'scan')
Inputs may be any that keep to these rules, and one draw needn't show every extreme that they name: slot_counts[t,s,s] = 2 for every band t and block column s; slots c < slot_counts[t,s,h] are the live ones.
All inputs are finite; a program needn't handle non-finite values.
Results may differ from a plain program's by a relative error of at most 0.011.
Values may be sent and summed in bfloat16 or wider, within the bound.
A program may use at most 128 MiB of HBM per device.

v0:
```python
import math

import jax
import jax.numpy as jnp
from jax import lax
from jax.sharding import PartitionSpec as P

step_size = 0.25
noise_scale = 0.5
amplitude_floor = 1.0


def with_halo(cells, sides, width):
    for axis, dim in sides:
        count = lax.axis_size(axis)
        ends = count - 1
        head = lax.slice_in_dim(cells, 0, width, axis=dim)
        tail = lax.slice_in_dim(cells, cells.shape[dim] - width, cells.shape[dim], axis=dim)
        cells = jnp.concatenate(
            [
                lax.ppermute(tail, axis, [(i, (i + 1) % count) for i in range(ends)]),
                cells,
                lax.ppermute(head, axis, [((i + 1) % count, i) for i in range(ends)]),
            ],
            axis=dim,
        )
    return cells


def dft_tables(width):
    index = jnp.arange(width, dtype=jnp.int32)
    phase = index[:, None] * index[None, :] % width
    angle = phase.astype(jnp.float32) * (2.0 * math.pi / width)
    norm = 1.0 / math.sqrt(width)
    return (
        (jnp.cos(angle) * norm).astype(jnp.bfloat16),
        (jnp.sin(angle) * norm).astype(jnp.bfloat16),
    )


def transform(stacked, cosine_table, sine_table, sign):
    count = stacked.shape[0]
    width = cosine_table.shape[0]
    signed_sine = (sign * sine_table.astype(jnp.float32)).astype(jnp.bfloat16)
    left_matrix = jnp.concatenate(
        [
            jnp.concatenate([cosine_table, signed_sine], 1),
            jnp.concatenate([-signed_sine, cosine_table], 1),
        ],
        0,
    )
    middle = jnp.einsum(
        "jk,nkl->njl", left_matrix, stacked, preferred_element_type=jnp.float32
    ).astype(jnp.bfloat16)
    middle = (
        middle.reshape(count, 2, width, width)
        .transpose(0, 2, 1, 3)
        .reshape(count, width, 2 * width)
    )
    right_matrix = jnp.concatenate(
        [
            jnp.concatenate([cosine_table, -signed_sine], 1),
            jnp.concatenate([signed_sine, cosine_table], 1),
        ],
        0,
    )
    result = jnp.einsum("njk,kl->njl", middle, right_matrix, preferred_element_type=jnp.float32)
    return (result[..., :width], result[..., width:])


def holder_gradients(patches, amps, probe_field, cosine_table, sine_table):
    probe_real, probe_imag = (probe_field[0], probe_field[1])
    patch_real = patches[:, 0].astype(jnp.float32)
    patch_imag = patches[:, 1].astype(jnp.float32)
    exit_real = (probe_real * patch_real - probe_imag * patch_imag).astype(jnp.bfloat16)
    exit_imag = (probe_real * patch_imag + probe_imag * patch_real).astype(jnp.bfloat16)
    far_real, far_imag = transform(
        jnp.concatenate([exit_real, exit_imag], 1), cosine_table, sine_table, 1.0
    )
    modulus = jnp.sqrt(far_real * far_real + far_imag * far_imag)
    keep = 1.0 - amps.astype(jnp.float32) / jnp.maximum(modulus, amplitude_floor)
    diff_real = (far_real * keep).astype(jnp.bfloat16)
    diff_imag = (far_imag * keep).astype(jnp.bfloat16)
    wave_real, wave_imag = transform(
        jnp.concatenate([diff_real, diff_imag], 1), cosine_table, sine_table, -1.0
    )
    grad_real = probe_real * wave_real + probe_imag * wave_imag
    grad_imag = probe_real * wave_imag - probe_imag * wave_real
    return jnp.stack([grad_real, grad_imag], 1).astype(jnp.bfloat16)


def cut_patches(source, rows, cols, width):

    def one(row, col):
        return lax.dynamic_slice(source, (jnp.int32(0), row, col), (source.shape[0], width, width))

    return jax.vmap(one)(rows, cols)


def add_patches(total, grads, rows, cols, live):

    def one_step(index, total):
        piece = grads[index].astype(jnp.float32) * live[index]
        start = (jnp.int32(0), rows[index], cols[index])
        current = lax.dynamic_slice(total, start, piece.shape)
        return lax.dynamic_update_slice(total, current + piece, start)

    return lax.fori_loop(0, grads.shape[0], one_step, total)


def fold_rims(rim_sums, axis, inner, half_patch):
    core = lax.slice_in_dim(rim_sums, 4 * half_patch // 2, 2 * half_patch + inner, axis=axis)
    upper = lax.slice_in_dim(rim_sums, 0, half_patch, axis=axis)
    lower = lax.slice_in_dim(rim_sums, inner + 3 * half_patch, inner + 4 * half_patch, axis=axis)
    upper_pad = [(0, 0)] * rim_sums.ndim
    lower_pad = [(0, 0)] * rim_sums.ndim
    upper_pad[axis] = (0, inner - half_patch)
    lower_pad[axis] = (inner - half_patch, 0)
    return core + jnp.pad(upper, upper_pad) + jnp.pad(lower, lower_pad)


def tap_stack(source, rows, cols):
    pieces = [
        source[:, shift_row : shift_row + rows, shift_col : shift_col + cols]
        for shift_row in range(3)
        for shift_col in range(3)
    ]
    return jnp.stack(pieces, 1).reshape(source.shape[0] * 9, rows, cols)


def hidden_units(taps, first_weight, first_bias, inside_mask):
    groups = (first_weight.reshape(4, -1, first_weight.shape[1]), first_bias.reshape(4, -1))

    def one_group(args):
        weight_part, bias_part = args
        pre = (
            jnp.einsum("ok,kyx->oyx", weight_part, taps, preferred_element_type=jnp.float32)
            + bias_part[:, None, None]
        )
        return (jax.nn.silu(pre) * inside_mask[None]).astype(jnp.bfloat16)

    stacked = lax.map(one_group, groups)
    return stacked.reshape(first_weight.shape[0], taps.shape[1], taps.shape[2])


def prior_terms(hidden_ext, second_weight, rows, cols):
    mixed = jnp.einsum("ko,oyx->kyx", second_weight, hidden_ext, preferred_element_type=jnp.float32)
    mixed = mixed.reshape(2, 9, rows + 2, cols + 2)
    total = jnp.zeros((2, rows, cols), jnp.float32)
    for shift_row in range(3):
        for shift_col in range(3):
            total = (
                total
                + mixed[
                    :,
                    shift_row * 3 + shift_col,
                    shift_row : shift_row + rows,
                    shift_col : shift_col + cols,
                ]
            )
    return total


def shards(
    specimen,
    sampler_noise,
    probe_field,
    amplitudes,
    corner_rows,
    corner_cols,
    slot_counts,
    first_weight,
    first_bias,
    second_weight,
    second_bias,
):
    patch_size = probe_field.shape[1]
    half_patch = patch_size // 2
    block_rows, block_cols = (specimen.shape[1], specimen.shape[2])
    peer_count = lax.axis_size("scan")
    capacity = corner_rows.shape[3]
    slot_total = peer_count * capacity
    cosine_table, sine_table = dft_tables(patch_size)
    specimen_bf = specimen.astype(jnp.bfloat16)
    rows_local = corner_rows[0, 0].reshape(slot_total)
    cols_local = corner_cols[0, 0].reshape(slot_total)
    held_amps = amplitudes[0, 0].reshape(slot_total, patch_size, patch_size)
    widened_rows = with_halo(specimen_bf, (("tile", 1),), half_patch)
    row_band = lax.all_gather(widened_rows, "scan", axis=2, tiled=True)
    row_band = jnp.pad(row_band, ((0, 0), (0, 0), (half_patch, half_patch)))
    wanted_rows, wanted_cols = (
        lax.all_to_all(corner_rows[0, 0], "scan", split_axis=0, concat_axis=0, tiled=True),
        lax.all_to_all(corner_cols[0, 0], "scan", split_axis=0, concat_axis=0, tiled=True),
    )
    owner_base = jnp.arange(peer_count, dtype=jnp.int32)[:, None] * block_cols
    patches = cut_patches(
        row_band,
        wanted_rows.reshape(slot_total),
        (owner_base + wanted_cols).reshape(slot_total),
        patch_size,
    )
    grads = holder_gradients(patches, held_amps, probe_field, cosine_table, sine_table)
    returned = lax.all_to_all(
        grads.reshape(peer_count, capacity, 2, patch_size, patch_size),
        "scan",
        split_axis=0,
        concat_axis=0,
        tiled=True,
    )
    returned = returned.reshape(slot_total, 2, patch_size, patch_size)
    live = (
        (jnp.arange(capacity, dtype=jnp.int32)[None, :] < slot_counts[0, 0][:, None])
        .astype(jnp.float32)
        .reshape(slot_total)
    )
    gradient_sum = jnp.zeros((2, block_rows + patch_size, block_cols + patch_size), jnp.float32)
    gradient_sum = add_patches(gradient_sum, returned, rows_local, cols_local, live)
    rim_sums = with_halo(
        gradient_sum.astype(jnp.bfloat16), (("tile", 1), ("scan", 2)), half_patch
    ).astype(gradient_sum.dtype)
    gradient = fold_rims(fold_rims(rim_sums, 1, block_rows, half_patch), 2, block_cols, half_patch)
    sampled = specimen - step_size * gradient + noise_scale * sampler_noise
    sampled_bf = sampled.astype(jnp.bfloat16)
    widened_input = with_halo(sampled_bf, (("tile", 1), ("scan", 2)), 2)
    total_rows = block_rows * lax.axis_size("tile")
    total_cols = block_cols * peer_count
    row_pos = lax.axis_index("tile") * block_rows - 1 + jnp.arange(block_rows + 2, dtype=jnp.int32)
    col_pos = lax.axis_index("scan") * block_cols - 1 + jnp.arange(block_cols + 2, dtype=jnp.int32)
    inside = ((row_pos >= 0) & (row_pos < total_rows))[:, None] & (
        (col_pos >= 0) & (col_pos < total_cols)
    )[None, :]
    hidden_ext = hidden_units(
        tap_stack(widened_input, block_rows + 2, block_cols + 2),
        first_weight,
        first_bias,
        inside.astype(jnp.float32),
    )
    prior_term = prior_terms(hidden_ext, second_weight, block_rows, block_cols)
    return sampled - (prior_term + second_bias[:, None, None])


def solution(mesh):
    return jax.shard_map(
        shards,
        mesh=mesh,
        in_specs=(
            P(None, "tile", "scan"),
            P(None, "tile", "scan"),
            P(),
            P("tile", "scan", None, None, None, None),
            P("tile", "scan", None, None),
            P("tile", "scan", None, None),
            P("tile", "scan", None),
            P(),
            P(),
            P(),
            P(),
        ),
        out_specs=P(None, "tile", "scan"),
        check_vma=False,
    )
```

profile of v0, /device:TPU:11, one launch (start us, length us, event | category | flops | bytes accessed | tf_op | source)
XLA Modules:
  0.0 1187.1 jit_solution(14024542501872576832)
XLA Ops:
  19.8 7.8 all-to-all-start.1
  34.7 7.2 all-to-all-start
  47.9 49.6 %all-gather.2.cloned.1.call-done = bf16[2,512,4096]{2,1,0:T(8,128)(2,1)} async-done(((bf16[2,512,256]{2,1,0:T(8,128)(2,1)}), bf16[2,512,4096]{2,1,0:T(8,128)(2,1)}) %all-gather.2.cloned.1.call-update) | async-done | bytes 8388624 | tf_op jit(solution)/shard_map/all_gather | solution.py:189
  97.5 7.5 pad.20
  105.0 126.6 %while.26 = (s32[]{:T(128)}, bf16[2,512,4352]{2,1,0:T(8,128)(2,1)}, s32[32,3]{0,1:T(4,128)S(1)}, bf16[32,2,256,256]{2,3,0,1:T(8,128)(2,1)}, s32[]{:T(128)}) while((s32[]{:T(128)}, bf16[2,512,4352]{2,1,0:T(8,128)(2,1)}, s32[32,3]{0,1:T(4,128)S(1)}, bf16[32,2,256,256]{2,3,0,1:T(8,128)(2,1)}, s32[]{:T(128)}) %tuple.75), condition=%wide.while_cond, body=%wide.while_body.sunk | while | flops 2 | bytes 1573489 | solution.py:95
  236.5 6.9 convert_bitcast_fusion.1
  243.4 12.6 %reshape.148 = bf16[32,2,256,256]{2,1,3,0:T(2,128)(2,1)} reshape(bf16[32,512,256]{1,2,0:T(8,128)(2,1)} %convert_bitcast_fusion.1) | data formatting | bytes 16777216 | tf_op jit(solution)/shard_map/reshape | solution.py:56
  255.9 28.8 %copy.116 = bf16[32,256,2,256]{3,2,1,0:T(2,128)(2,1)} copy(bf16[32,256,2,256]{1,2,3,0:T(2,128)(2,1)} %bitcast.222) | data formatting | bytes 16777216 | tf_op jit(solution)/shard_map/transpose | solution.py:57
  284.7 14.0 %reshape.149 = bf16[32,256,512]{2,1,0:T(8,128)(2,1)} reshape(bf16[32,256,2,256]{3,2,1,0:T(2,128)(2,1)} %copy.116) | data formatting | bytes 16777216 | tf_op jit(solution)/shard_map/reshape | solution.py:58
  298.7 7.4 fusion.30
  306.2 7.4 multiply_convert_fusion.2
  313.6 9.3 convert_bitcast_fusion
  322.8 12.5 %reshape.150 = bf16[32,2,256,256]{2,1,3,0:T(2,128)(2,1)} reshape(bf16[32,512,256]{1,2,0:T(8,128)(2,1)} %convert_bitcast_fusion) | data formatting | bytes 16777216 | tf_op jit(solution)/shard_map/reshape | solution.py:56
  335.4 28.7 %copy.118 = bf16[32,256,2,256]{3,2,1,0:T(2,128)(2,1)} copy(bf16[32,256,2,256]{1,2,3,0:T(2,128)(2,1)} %bitcast.223) | data formatting | bytes 16777216 | tf_op jit(solution)/shard_map/transpose | solution.py:57
  364.1 14.0 %reshape.151 = bf16[32,256,512]{2,1,0:T(8,128)(2,1)} reshape(bf16[32,256,2,256]{3,2,1,0:T(2,128)(2,1)} %copy.118) | data formatting | bytes 16777216 | tf_op jit(solution)/shard_map/reshape | solution.py:58
  378.1 13.1 %fusion.37 = f32[32,256,512]{1,2,0:T(8,128)} fusion(bf16[32,256,512]{2,1,0:T(8,128)(2,1)} %reshape.151, bf16[256,256]{1,0:T(8,128)(2,1)S(1)} %get-tuple-element.256, bf16[256,256]{1,0:T(8,128)(2,1)S(1)} %multiply_convert_fusion.3, bf16[256,256]{1,0:T(8,128)(2,1)S(1)} %fusion.79), kind=kOutput, calls=%fused_computation.60 | convolution fusion | flops 4297064448 | bytes 25559040 | tf_op jit(solution)/shard_map/njk,kl->njl/dot_general | solution.py:67
  391.2 8.7 add_convert_fusion
  399.9 6.2 pad_maximum_fusion
  406.1 5.3 all-to-all-start.2
  411.9 99.9 %all-to-all-done.2 = bf16[16,2,2,256,256]{3,4,1,2,0:T(8,128)(2,1)} async-done(((bf16[16,2,2,256,256]{3,4,1,2,0:T(8,128)(2,1)}), bf16[16,2,2,256,256]{3,4,1,2,0:T(8,128)(2,1)}, u32[]{:S(2)}, u32[]{:S(2)}) %all-to-all-start.2) | async-done | bytes 8388640 | tf_op jit(solution)/shard_map/all_to_all | solution.py:203
  511.9 12.3 %copy.123 = bf16[16,2,2,256,256]{4,3,2,1,0:T(8,128)(2,1)} copy(bf16[16,2,2,256,256]{3,4,1,2,0:T(8,128)(2,1)} %all-to-all-done.2) | data formatting | bytes 16777216 | tf_op jit(solution)/shard_map/all_to_all | solution.py:203
  524.4 525.9 %while.25 = (s32[]{:T(128)}, f32[2,512,512]{2,1,0:T(8,128)S(1)}, s32[32]{0:T(128)S(1)}, s32[32]{0:T(128)S(1)}, bf16[32,2,256,256]{3,2,1,0:T(8,128)(2,1)}, /*inde...) while((s32[]{:T(128)}, f32[2,512,512]{2,1,0:T(8,128)S(1)}, s32[32]{0:T(128)S(1)}, s32[32]{0:T(128)S(1)}, ...), condition=%wide.region_1.2_spmd, body=%wide.region_0.1_spmd.sunk | while | flops 393224 | bytes 2359513 | solution.py:108
  532.0 9.5 dynamic_update_slice.15
  549.0 8.4 dynamic_update_slice.15
  565.0 9.8 dynamic_update_slice.15
  582.5 9.2 dynamic_update_slice.15
  599.2 8.8 dynamic_update_slice.15
  615.6 8.5 dynamic_update_slice.15
  631.6 7.3 dynamic_update_slice.15
  646.6 7.9 dynamic_update_slice.15
  662.0 7.9 dynamic_update_slice.15
  677.5 9.5 dynamic_update_slice.15
  694.7 9.1 dynamic_update_slice.15
  711.4 9.2 dynamic_update_slice.15
  728.2 10.7 dynamic_update_slice.15
  746.4 7.9 dynamic_update_slice.15
  762.0 8.1 dynamic_update_slice.15
  777.7 9.9 dynamic_update_slice.15
  795.2 8.3 dynamic_update_slice.15
  811.1 9.4 dynamic_update_slice.15
  828.1 10.1 dynamic_update_slice.15
  845.8 8.9 dynamic_update_slice.15
  862.4 8.5 dynamic_update_slice.15
  878.4 9.9 dynamic_update_slice.15
  895.9 7.0 dynamic_update_slice.15
  910.6 8.9 dynamic_update_slice.15
  927.0 8.4 dynamic_update_slice.15
  943.0 8.2 dynamic_update_slice.15
  958.8 8.3 dynamic_update_slice.15
  974.7 9.3 dynamic_update_slice.15
  991.6 9.1 dynamic_update_slice.15
  1008.3 9.8 dynamic_update_slice.15
  1025.7 8.3 dynamic_update_slice.15
  1041.6 8.7 dynamic_update_slice.15
  1050.5 9.7 collective-permute-start.2
  1070.2 31.9 %collective-permute-start.5 = (bf16[2,768,128]{2,1,0:T(8,128)(2,1)S(1)}, bf16[2,768,128]{2,1,0:T(8,128)(2,1)S(1)}, u32[]{:S(2)}, u32[]{:S(2)}) collective-permute-start(bf16[2,768,128]{2,1,0:T(8,128)(2,1)S(1)} %get-tuple-element.240), channel_id=1, source_target_pairs={{1,0},{2,1},{3,2},{4,3},{5,4},{6,5},{7,6},{8,7},{9,8},{10,9},{11,1... | collective-permute-start | bytes 1179656 | tf_op jit(solution)/shard_map/ppermute | solution.py:23
  1102.1 6.2 collective-permute-done.4
  1119.9 5.9 collective-permute-start.9
  1134.0 32.9 %while.27 = (s32[]{:T(128)}, bf16[4,32,258,258]{3,1,0,2:T(8,128)(2,1)}, bf16[4,32,18]{1,2,0:T(8,128)(2,1)S(1)}, bf16[18,258,258]{2,0,1:T(8,128)(2,1)}, f32[4,32]...) while((s32[]{:T(128)}, ...), condition=%wide.region_3.4_spmd.clone, body=%wide.region_2.3_spmd.clone.sunk | while | flops 91725192 | bytes 11776365 | solution.py:142
  1134.2 8.2 bitcast_dynamic-update-slice_fusion.2
  1142.5 8.0 bitcast_dynamic-update-slice_fusion.2
  1150.6 8.1 bitcast_dynamic-update-slice_fusion.2
  1158.8 8.1 bitcast_dynamic-update-slice_fusion.2
  1166.9 10.0 convolution_bitcast_fusion
  (400 shorter events, 311.2 us)
Async XLA Ops:
  6.5 1160.4 %copy-start = (bf16[18,128]{1,0:T(8,128)(2,1)S(1)}, bf16[18,128]{1,0:T(8,128)(2,1)}, u32[]{:S(2)}) copy-start(bf16[18,128]{1,0:T(8,128)(2,1)} %param.24) | copy-start | bytes 13828
  6.5 91.0 %all-gather.2.cloned.1.call-start = ((), (), s32[]{:S(2)}) async-start(), calls=%async_computation.3 | async-start | bytes 8912896 | tf_op jit(solution)/shard_map/all_gather | solution.py:189
  7.6 5.6 collective-permute-start
  11.3 6.3 collective-permute-start.1
  19.8 14.9 %all-to-all-start.1 = ((s32[16,1,2]{2,1,0:T(1,128)}), s32[16,1,2]{2,1,0:T(1,128)S(1)}, u32[]{:S(2)}, u32[]{:S(2)}) async-start(s32[16,1,2]{2,1,0:T(1,128)} %copy.112), calls=%async_computation.1 | async-start | bytes 16384 | tf_op jit(solution)/shard_map/all_to_all | solution.py:193
  34.7 12.5 %all-to-all-start = ((s32[16,1,2]{2,1,0:T(1,128)}), s32[16,1,2]{2,1,0:T(1,128)S(1)}, u32[]{:S(2)}, u32[]{:S(2)}) async-start(s32[16,1,2]{2,1,0:T(1,128)} %copy.111), calls=%async_computation | async-start | bytes 16384 | tf_op jit(solution)/shard_map/all_to_all | solution.py:192
  298.7 7.4 copy-start.1
  406.1 5.3 copy-start.5
  406.1 5.3 copy-start.6
  406.1 5.4 copy-start.9
  406.1 105.7 %all-to-all-start.2 = ((bf16[16,2,2,256,256]{3,4,1,2,0:T(8,128)(2,1)}), bf16[16,2,2,256,256]{3,4,1,2,0:T(8,128)(2,1)}, u32[]{:S(2)}, u32[]{:S(2)}) async-start(bf16[16,2,2,256,256]{3,4,1,2,0:T(8,128)(2,1)} %pad_maximum_fusion), calls=%async_computation.2 | async-start | bytes 16777216 | tf_op jit(solution)/shard_map/all_to_all | solution.py:203
  1050.3 60.2 %copy-start.7 = (pred[256]{0:T(512)(128)(4,1)S(1)}, pred[256]{0:T(512)(128)(4,1)}, u32[]{:S(2)}) copy-start(pred[256]{0:T(512)(128)(4,1)} %constant.95.clone.1) | copy-start | bytes 772
  1050.5 13.0 %collective-permute-start.2 = (bf16[2,128,512]{2,1,0:T(8,128)(2,1)S(1)}, bf16[2,128,512]{2,1,0:T(8,128)(2,1)S(1)}, u32[]{:S(2)}, u32[]{:S(2)}) collective-permute-start(bf16[2,128,512]{2,1,0:T(8,128)(2,1)S(1)} %get-tuple-element.241), channel_id=1, source_target_pairs={{0,16},{16,32},{32,48},{48,64},{64,80},{80,96},{96,112},{1,17},{17... | collective-permute-start | bytes 786440 | tf_op jit(solution)/shard_map/ppermute | solution.py:21
  1060.2 7.7 collective-permute-start.3
  1068.1 42.7 %copy-start.2 = (f32[2,256,256]{2,1,0:T(8,128)S(1)}, f32[2,256,256]{2,1,0:T(8,128)}, u32[]{:S(2)}) copy-start(f32[2,256,256]{2,1,0:T(8,128)} %param.15) | copy-start | bytes 1572868
  1068.1 42.7 %copy-start.3 = (f32[2,256,256]{2,1,0:T(8,128)S(1)}, f32[2,256,256]{2,1,0:T(8,128)}, u32[]{:S(2)}) copy-start(f32[2,256,256]{2,1,0:T(8,128)} %param.16) | copy-start | bytes 1572868
  1068.1 40.2 %collective-permute-start.4 = (bf16[2,768,128]{2,1,0:T(8,128)(2,1)S(1)}, bf16[2,768,128]{2,1,0:T(8,128)(2,1)S(1)}, u32[]{:S(2)}, u32[]{:S(2)}) collective-permute-start(bf16[2,768,128]{2,1,0:T(8,128)(2,1)S(1)} %get-tuple-element.239), channel_id=1, source_target_pairs={{0,1},{1,2},{2,3},{3,4},{4,5},{5,6},{6,7},{7,8},{8,9},{9,10},{10,1... | collective-permute-start | bytes 1179656 | tf_op jit(solution)/shard_map/ppermute | solution.py:21
  1070.2 39.9 %collective-permute-start.5 = (bf16[2,768,128]{2,1,0:T(8,128)(2,1)S(1)}, bf16[2,768,128]{2,1,0:T(8,128)(2,1)S(1)}, u32[]{:S(2)}, u32[]{:S(2)}) collective-permute-start(bf16[2,768,128]{2,1,0:T(8,128)(2,1)S(1)} %get-tuple-element.240), channel_id=1, source_target_pairs={{1,0},{2,1},{3,2},{4,3},{5,4},{6,5},{7,6},{8,7},{9,8},{10,9},{11,1... | collective-permute-start | bytes 1179656 | tf_op jit(solution)/shard_map/ppermute | solution.py:23
  1110.1 15.8 %copy-start.4 = (bf16[128,18]{0,1:T(8,128)(2,1)S(1)}, bf16[128,18]{0,1:T(8,128)(2,1)}, u32[]{:S(2)}) copy-start(bf16[128,18]{0,1:T(8,128)(2,1)} %param.22) | copy-start | bytes 13828
  1110.1 15.9 %copy-start.10 = (f32[128]{0:T(128)S(1)}, f32[128]{0:T(128)}, u32[]{:S(2)}) copy-start(f32[128]{0:T(128)} %param.23) | copy-start | bytes 1540
  1111.0 4.6 collective-permute-start.6
  1112.9 4.9 collective-permute-start.7
  1118.0 10.0 collective-permute-start.8
  1119.9 9.1 collective-permute-start.9
  1176.9 1.4 copy-start.8
Sparse Core Ops, SparseCore 0:
  18.6 78.9 all-gather.1
where the time goes:
time: 1210 us; the launch traced here: 1190 us
  local copies, waits for them, and re-layouts  614 us (51%)
  waiting for transfers between devices  177 us (15%)
  loops' own time  123 us (10%)
  other arithmetic  95.9 us (8%)
  starting transfers between devices  83.9 us (7%)
  matrix products  79.1 us (7%)
  between operations  14.2 us (1%)
    dynamic_update_slice x32, local copies, waits for them, and re-layouts, one_step(): return lax.dynamic_update_slice(total, current + piece, start)  283 us
    gather x160, local copies, waits for them, and re-layouts  126 us
    another operation x1, loops' own time, add_patches(): return lax.fori_loop(0, grads.shape[0], one_step, total)  123 us
    all_to_all x1, waiting for transfers between devices, shards(): lax.all_to_all(grads.reshape(peer_count, capacity, 2, patch_size, patch_s...  99.9 us
    add x32, other arithmetic, one_step(): return lax.dynamic_update_slice(total, current + piece, start)  57.5 us
    transpose x2, local copies, waits for them, and re-layouts, transform(): middle = middle.reshape(count, 2, width, width).transpose(0, 2, 1, 3).res...  57.5 us
    all_gather x1, waiting for transfers between devices, shards(): row_band = lax.all_gather(widened_rows, 'scan', axis=2, tiled=True)  49.6 us
    ppermute x5, starting transfers between devices, with_halo(): lax.ppermute(head, axis, [((i + 1) % count, i) for i in range(ends)])  44.3 us
  transfers between devices with their start and end apart: 14, of which 11 were waited for; matrix products, arithmetic and copies ran while one was open for 1% of the time, Pallas kernels for 0%

commit v1 on v0

v1 whole, which is shorter than its diff:
```python
import functools

import jax
import jax.numpy as jnp
import numpy as np
from jax import lax
from jax.experimental import pallas as pl
from jax.experimental.pallas import tpu as pltpu
from jax.sharding import PartitionSpec as P

MESH = pl.DeviceIdType.MESH
NW = 256
HALF = 128
EDGE = 16
WIDE = 384
CAP = 2

ORDER_16 = [(0, 3), (1, 0), (3, 2), (3, 1), (3, 3), (0, 2), (1, 3), (2, 0), (0, 1), (2, 1), (2, 3), (1, 2), (3, 0), (1, 1), (2, 2)]
SIDES = [(a, b) for a in (-1, 0, 1) for b in (-1, 0, 1) if (a, b) != (0, 0)]


def dft_matrices():
    index = np.arange(NW)
    angle = (index[:, None] * index[None, :] % NW) * (2.0 * np.pi / NW)
    cosine = (np.cos(angle) / 16.0).astype(jnp.bfloat16)
    sine = (np.sin(angle) / 16.0).astype(jnp.bfloat16)
    forward = np.concatenate([np.concatenate([cosine, sine], 1), np.concatenate([-sine, cosine], 1)], 0)
    return forward, np.ascontiguousarray(forward.T)


def span(step, low, mid, high):
    return {-1: low, 0: mid, 1: high}[step]


def patch_kernel(
    order, rows_y, tiles, peers,
    rows_ref, cols_ref, counts_ref, amps_ref, spec_ref, noise_ref, probe_ref, fwd_ref, inv_ref,
    out_ref, cells_ref,
    recv, frame, acc, rim, rim_in, probe2, rolled, wave_in, mid_ref, far_ref,
    amp_send, amp_recv, own_sem, halo_send, halo_recv, rim_send, rim_recv, ring_send, ring_recv,
):
    f32, bf16 = jnp.float32, jnp.bfloat16
    t = lax.axis_index("tile")
    s = lax.axis_index("scan")
    rows_z = peers // rows_y
    y, z = s // rows_z, lax.rem(s, rows_z)

    def peer(dy, dz):
        return lax.rem(y + dy + rows_y, rows_y) * rows_z + lax.rem(z + dz + rows_z, rows_z)

    def exists(dt, ds):
        ok_t = {-1: t > 0, 0: t >= 0, 1: t < tiles - 1}[dt]
        ok_s = {-1: s > 0, 0: s >= 0, 1: s < peers - 1}[ds]
        return jnp.logical_and(ok_t, ok_s)

    barrier = pltpu.get_barrier_semaphore()
    expected = jnp.int32(len(order))
    for dy, dz in order:
        pl.semaphore_signal(barrier, inc=1, device_id=(t, peer(-dy, -dz)), device_id_type=MESH)
    for dt, ds in SIDES:
        if dt != 0:
            here = exists(dt, ds)
            expected = expected + here.astype(jnp.int32)

            @pl.when(here)
            def _():
                pl.semaphore_signal(barrier, inc=1, device_id=(t + dt, s + ds), device_id_type=MESH)

    own = pltpu.make_async_copy(amps_ref.at[s], recv.at[0], own_sem)
    own.start()
    for part in range(2):
        frame[part, HALF : HALF + NW, HALF : HALF + NW] = spec_ref[part].astype(bf16)
    pl.semaphore_wait(barrier, expected)

    def halo_copy(k, dt, ds):
        src = (slice(None), slice(*span(dt, (128, 256), (128, 384), (256, 384))), slice(*span(ds, (128, 256), (128, 384), (256, 384))))
        dst = (slice(None), slice(*span(dt, (384, 512), (128, 384), (0, 128))), slice(*span(ds, (384, 512), (128, 384), (0, 128))))
        return pltpu.make_async_remote_copy(
            src_ref=frame.at[src], dst_ref=frame.at[dst], send_sem=halo_send.at[k], recv_sem=halo_recv.at[k],
            device_id=(t + dt, s + ds), device_id_type=MESH,
        )

    def amp_copy(k, dy, dz):
        d = peer(dy, dz)
        return pltpu.make_async_remote_copy(
            src_ref=amps_ref.at[d], dst_ref=recv.at[k], send_sem=amp_send.at[k], recv_sem=amp_recv.at[k],
            device_id=(t, d), device_id_type=MESH,
        )

    for k, (dt, ds) in enumerate(SIDES):
        @pl.when(exists(dt, ds))
        def _():
            halo_copy(k, dt, ds).start()
    for k, (dy, dz) in enumerate(order):
        amp_copy(k + 1, dy, dz).start()

    for part in range(2):
        acc[part] = jnp.zeros((2 * NW, 2 * NW), f32)
        acc[part, HALF : HALF + NW, HALF : HALF + NW] = spec_ref[part] + 0.5 * noise_ref[part]
        for half in range(2):
            columns = probe_ref[part, :, half * HALF : (half + 1) * HALF]
            probe2[part, half, :NW, :] = columns
            probe2[part, half, NW:, :] = columns

    for k, (dt, ds) in enumerate(SIDES):
        here = exists(-dt, -ds)

        @pl.when(here)
        def _():
            halo_copy(k, dt, ds).wait_recv()

        @pl.when(jnp.logical_not(here))
        def _():
            at_row, at_col = span(dt, (384, 512), (128, 384), (0, 128)), span(ds, (384, 512), (128, 384), (0, 128))
            for part in range(2):
                frame[part, slice(*at_row), slice(*at_col)] = jnp.zeros((at_row[1] - at_row[0], at_col[1] - at_col[0]), bf16)

    own.wait()

    def step(k, carry):
        dy, dz = jnp.int32(0), jnp.int32(0)
        for i, (a, b) in enumerate(order):
            dy = jnp.where(k == i + 1, a, dy)
            dz = jnp.where(k == i + 1, b, dz)
        h = peer(-dy, -dz)
        corner = [(rows_ref[h * CAP + c], cols_ref[h * CAP + c]) for c in range(CAP)]
        scale = [jnp.where(counts_ref[h] > c, f32(-0.25), f32(0.0)) for c in range(CAP)]
        CH = 32
        lane = lax.broadcasted_iota(jnp.int32, (CH, NW), 1)
        sub = lax.broadcasted_iota(jnp.int32, (CH, NW), 0)

        def exits(i, carry):
            base = pl.multiple_of(i * CH, CH)
            for c in range(CAP):
                r, q = corner[c]
                low_row = sub + base < r
                low_col = lane < q
                shift = lax.rem(q, NW)
                cell, prb = [], []
                for part in range(2):
                    tile = [[frame[part, pl.ds(base + a * NW, CH), b * NW : (b + 1) * NW].astype(f32) for b in range(2)] for a in range(2)]
                    cell.append(jnp.where(low_row, jnp.where(low_col, tile[1][1], tile[1][0]), jnp.where(low_col, tile[0][1], tile[0][0])))
                    turned = pltpu.roll(jnp.concatenate([probe2[part, half, pl.ds(base + NW - r, CH), :] for half in range(2)], 1), shift, 1)
                    rolled[c, part, pl.ds(base, CH), :] = turned
                    prb.append(turned)
                wave_in[pl.ds(base, CH), c * NW : (c + 1) * NW] = (prb[0] * cell[0] - prb[1] * cell[1]).astype(bf16)
                wave_in[pl.ds(base + NW, CH), c * NW : (c + 1) * NW] = (prb[0] * cell[1] + prb[1] * cell[0]).astype(bf16)
            return carry

        lax.fori_loop(0, NW // CH, exits, 0)

        def both(left_ref, right_ref):
            for c in range(CAP):
                mid = jnp.dot(left_ref[...], wave_in[:, c * NW : (c + 1) * NW], preferred_element_type=f32)
                for p in range(2):
                    mid_ref[c * NW : (c + 1) * NW, p * NW : (p + 1) * NW] = mid[p * NW : (p + 1) * NW].astype(bf16)
            for p in range(2):
                far_ref[:, p * NW : (p + 1) * NW] = jnp.dot(mid_ref[...], right_ref[:, p * NW : (p + 1) * NW], preferred_element_type=f32)

        both(fwd_ref, inv_ref)

        @pl.when(k > 0)
        def _():
            pltpu.make_async_remote_copy(
                src_ref=recv.at[k], dst_ref=recv.at[k], send_sem=amp_send.at[k], recv_sem=amp_recv.at[k],
                device_id=(t, peer(dy, dz)), device_id_type=MESH,
            ).wait_recv()

        def correct(i, carry):
            base = pl.multiple_of(i * CH, CH)
            for c in range(CAP):
                fr = far_ref[pl.ds(base + c * NW, CH), :NW]
                fi = far_ref[pl.ds(base + c * NW, CH), NW:]
                amp = recv[k, c, pl.ds(base, CH), :].astype(f32)
                keep = 1.0 - amp * lax.rsqrt(jnp.maximum(fr * fr + fi * fi, 1.0))
                wave_in[pl.ds(base, CH), c * NW : (c + 1) * NW] = (fr * keep).astype(bf16)
                wave_in[pl.ds(base + NW, CH), c * NW : (c + 1) * NW] = (fi * keep).astype(bf16)
            return carry

        lax.fori_loop(0, NW // CH, correct, 0)
        both(inv_ref, fwd_ref)

        def gather(i, carry):
            base = pl.multiple_of(i * CH, CH)
            grads = []
            for c in range(CAP):
                wr = far_ref[pl.ds(base + c * NW, CH), :NW]
                wi = far_ref[pl.ds(base + c * NW, CH), NW:]
                pr = rolled[c, 0, pl.ds(base, CH), :] * scale[c]
                pi = rolled[c, 1, pl.ds(base, CH), :] * scale[c]
                grads.append((pr * wr + pi * wi, pr * wi - pi * wr))
            for a in range(2):
                for b in range(2):
                    masks = []
                    for c in range(CAP):
                        r, q = corner[c]
                        row_ok = sub + base < r if a else sub + base >= r
                        col_ok = lane < q if b else lane >= q
                        masks.append(jnp.logical_and(row_ok, col_ok))
                    for part in range(2):
                        total = acc[part, pl.ds(base + a * NW, CH), b * NW : (b + 1) * NW]
                        for c in range(CAP):
                            total = total + jnp.where(masks[c], grads[c][part], 0.0)
                        acc[part, pl.ds(base + a * NW, CH), b * NW : (b + 1) * NW] = total
            return carry

        lax.fori_loop(0, NW // CH, gather, 0)
        return carry

    lax.fori_loop(0, len(order) + 1, step, 0)

    for part in range(2):
        for lo, hi in ((0, HALF), (HALF + NW, 2 * NW)):
            rim[part, lo:hi, :] = acc[part, lo:hi, :].astype(bf16)
            rim[part, HALF : HALF + NW, lo:hi] = acc[part, HALF : HALF + NW, lo:hi].astype(bf16)

    def rim_copy(k, dt, ds):
        where = (slice(None), slice(*span(dt, (0, 128), (128, 384), (384, 512))), slice(*span(ds, (0, 128), (128, 384), (384, 512))))
        return pltpu.make_async_remote_copy(
            src_ref=rim.at[where], dst_ref=rim_in.at[where], send_sem=rim_send.at[k], recv_sem=rim_recv.at[k],
            device_id=(t + dt, s + ds), device_id_type=MESH,
        )

    for k, (dt, ds) in enumerate(SIDES):
        @pl.when(exists(dt, ds))
        def _():
            rim_copy(k, dt, ds).start()
    for part in range(2):
        out_ref[part] = acc[part, HALF : HALF + NW, HALF : HALF + NW]
    for k, (dt, ds) in enumerate(SIDES):
        @pl.when(exists(-dt, -ds))
        def _():
            rim_copy(k, dt, ds).wait_recv()
            src_r, dst_r = span(dt, ((0, 128), (128, 256)), ((128, 384), (0, 256)), ((384, 512), (0, 128)))
            src_c, dst_c = span(ds, ((0, 128), (128, 256)), ((128, 384), (0, 256)), ((384, 512), (0, 128)))
            for part in range(2):
                out_ref[part, slice(*dst_r), slice(*dst_c)] += rim_in[part, slice(*src_r), slice(*src_c)].astype(f32)
    for part in range(2):
        cells_ref[part, EDGE : EDGE + NW, HALF : HALF + NW] = out_ref[part].astype(bf16)

    def ring_copy(k, dt, ds):
        src = (slice(None), slice(*span(dt, (16, 32), (16, 272), (256, 272))), slice(*span(ds, (128, 256), (128, 384), (256, 384))))
        dst = (slice(None), slice(*span(dt, (272, 288), (16, 272), (0, 16))), slice(*span(ds, (384, 512), (128, 384), (0, 128))))
        return pltpu.make_async_remote_copy(
            src_ref=cells_ref.at[src], dst_ref=cells_ref.at[dst], send_sem=ring_send.at[k], recv_sem=ring_recv.at[k],
            device_id=(t + dt, s + ds), device_id_type=MESH,
        )

    for k, (dt, ds) in enumerate(SIDES):
        @pl.when(exists(dt, ds))
        def _():
            ring_copy(k, dt, ds).start()
    for k, (dt, ds) in enumerate(SIDES):
        here = exists(-dt, -ds)

        @pl.when(here)
        def _():
            ring_copy(k, dt, ds).wait_recv()

        @pl.when(jnp.logical_not(here))
        def _():
            at_row, at_col = span(dt, (272, 288), (16, 272), (0, 16)), span(ds, (384, 512), (128, 384), (0, 128))
            for part in range(2):
                cells_ref[part, slice(*at_row), slice(*at_col)] = jnp.zeros((at_row[1] - at_row[0], at_col[1] - at_col[0]), bf16)

    for k, (dt, ds) in enumerate(SIDES):
        @pl.when(exists(dt, ds))
        def _():
            ring_copy(k, dt, ds).wait_send()
            halo_copy(k, dt, ds).wait_send()
            rim_copy(k, dt, ds).wait_send()
    for k, (dy, dz) in enumerate(order):
        amp_copy(k + 1, dy, dz).wait_send()


def sample(specimen, noise, probe, amps, rows, cols, counts):
    tiles, peers = lax.axis_size("tile"), lax.axis_size("scan")
    if peers == 16:
        order, rows_y = ORDER_16, 4
    else:
        order, rows_y = [(0, b) for b in range(1, peers)], 1
    forward, inverse = dft_matrices()
    f32, bf16 = jnp.float32, jnp.bfloat16
    smem = pl.BlockSpec(memory_space=pltpu.SMEM)
    vmem = pl.BlockSpec(memory_space=pltpu.VMEM)
    dma = pltpu.SemaphoreType.DMA
    return pl.pallas_call(
        functools.partial(patch_kernel, order, rows_y, tiles, peers),
        out_shape=(jax.ShapeDtypeStruct((2, NW, NW), f32), jax.ShapeDtypeStruct((2, NW + 2 * EDGE, 2 * NW), bf16)),
        in_specs=[smem, smem, smem, pl.BlockSpec(memory_space=pl.ANY), vmem, vmem, vmem, vmem, vmem],
        out_specs=(vmem, vmem),
        scratch_shapes=[
            pltpu.VMEM((peers, CAP, NW, NW), bf16),
            pltpu.VMEM((2, 2 * NW, 2 * NW), bf16),
            pltpu.VMEM((2, 2 * NW, 2 * NW), f32),
            pltpu.VMEM((2, 2 * NW, 2 * NW), bf16),
            pltpu.VMEM((2, 2 * NW, 2 * NW), bf16),
            pltpu.VMEM((2, 2, 2 * NW, HALF), f32),
            pltpu.VMEM((CAP, 2, NW, NW), f32),
            pltpu.VMEM((2 * NW, 2 * NW), bf16),
            pltpu.VMEM((2 * NW, 2 * NW), bf16),
            pltpu.VMEM((2 * NW, 2 * NW), f32),
            dma((peers,)), dma((peers,)), dma, dma((8,)), dma((8,)), dma((8,)), dma((8,)), dma((8,)), dma((8,)),
        ],
        compiler_params=pltpu.CompilerParams(collective_id=0, has_side_effects=True, vmem_limit_bytes=48 << 20),
        name="patches",
    )(rows, cols, counts, amps, specimen, noise, probe, jnp.asarray(forward), jnp.asarray(inverse))


def tap_selectors():
    first = np.zeros((18, 24), np.float32)
    second = np.zeros((24, 18), np.float32)
    for c in range(2):
        for dy in range(3):
            for dx in range(3):
                first[9 * c + 3 * dy + dx, 8 * dy + 3 * c + dx] = 0.5
                second[8 * dy + 3 * c + dx, 9 * c + 3 * dy + dx] = 1.0
    return first.astype(jnp.bfloat16), second.astype(jnp.bfloat16)


def prior_kernel(
    tiles, peers, cells_ref, sampled_ref, w1_ref, b1_ref, w2_ref, b2_ref, sel1_ref, sel2_ref, out_ref, taps, mixed_sum,
):
    f32, bf16 = jnp.float32, jnp.bfloat16
    t = lax.axis_index("tile")
    s = lax.axis_index("scan")
    rows = NW + 2 * EDGE
    square = lax.broadcasted_iota(jnp.int32, (128, 128), 0) == lax.broadcasted_iota(jnp.int32, (128, 128), 1)
    bias = jnp.sum(jnp.where(square, b1_ref[...], 0.0), axis=1, keepdims=True) * 0.5
    high = bias.astype(bf16).astype(f32)
    column = lax.broadcasted_iota(jnp.int32, (128, 24), 1)
    first = jnp.dot(w1_ref[...], sel1_ref[...], preferred_element_type=f32)
    first = (first + jnp.where(column == 6, high, 0.0) + jnp.where(column == 7, bias - high, 0.0)).astype(bf16)
    second = jnp.dot(sel2_ref[...], w2_ref[...], preferred_element_type=f32).astype(bf16)

    for c in range(2):
        plane = cells_ref[c].astype(f32)
        for dx in range(3):
            moved = pltpu.roll(plane, 2 * NW - (126 + dx), 1)
            for v in range(3):
                taps[v, pl.ds(3 * c + dx, rows, stride=8), :] = moved[:, v * 128 : (v + 1) * 128]
    for v in range(3):
        for k in (6, 7):
            taps[v, pl.ds(k, rows, stride=8), :] = jnp.ones((rows, 128), f32)

    lane = lax.broadcasted_iota(jnp.int32, (24, WIDE), 1)
    inside = jnp.logical_and(jnp.logical_or(lane > 0, s > 0), jnp.logical_or(lane < NW + 1, s < peers - 1))
    GROUP = 6

    def group(g, carry):
        older, old = carry
        for j in range(GROUP):
            index = g * GROUP + j
            start = pl.multiple_of((index + EDGE - 2) * 8, 8)
            window = jnp.concatenate([taps[v, pl.ds(start, 24), :] for v in range(3)], 1).astype(bf16)
            pre = jnp.dot(first, window, preferred_element_type=f32)
            hidden = (pre + pre * jnp.tanh(pre)).astype(bf16)
            here = jnp.logical_and(jnp.logical_or(index > 0, t > 0), jnp.logical_or(index < NW + 1, t < tiles - 1))
            mixed = jnp.where(jnp.logical_and(inside, here), jnp.dot(second, hidden, preferred_element_type=f32), 0.0)
            done = older + mixed[16:24]
            for v in range(3):
                mixed_sum[v, pl.ds(pl.multiple_of(index * 8, 8), 8), :] = done[:, v * 128 : (v + 1) * 128]
            older = old + mixed[8:16]
            old = mixed[0:8]
        return older, old

    zero = jnp.zeros((8, WIDE), f32)
    lax.fori_loop(0, (NW + 2) // GROUP, group, (zero, zero))
    for c in range(2):
        total = None
        for dx in range(3):
            part = jnp.concatenate([mixed_sum[v, pl.ds(16 + 3 * c + dx, NW, stride=8), :] for v in range(3)], 1)
            part = (pltpu.roll(part, WIDE - dx, 1) if dx else part)[:, :NW]
            total = part if total is None else total + part
        out_ref[c] = sampled_ref[c] - (total + b2_ref[c])


def subtract_prior(cells, sampled, first_weight, first_bias, second_weight, second_bias):
    tiles, peers = lax.axis_size("tile"), lax.axis_size("scan")
    f32 = jnp.float32
    smem = pl.BlockSpec(memory_space=pltpu.SMEM)
    vmem = pl.BlockSpec(memory_space=pltpu.VMEM)
    one, two = tap_selectors()
    return pl.pallas_call(
        functools.partial(prior_kernel, tiles, peers),
        out_shape=jax.ShapeDtypeStruct((2, NW, NW), f32),
        in_specs=[vmem, vmem, vmem, vmem, vmem, smem, vmem, vmem],
        out_specs=vmem,
        scratch_shapes=[
            pltpu.VMEM((3, 8 * (NW + 2 * EDGE), 128), f32),
            pltpu.VMEM((3, 8 * (NW + 2), 128), f32),
        ],
        compiler_params=pltpu.CompilerParams(vmem_limit_bytes=32 << 20),
        name="prior",
    )(cells, sampled, first_weight, first_bias.reshape(1, -1), second_weight, second_bias, jnp.asarray(one), jnp.asarray(two))


def shards(
    specimen, sampler_noise, probe_field, amplitudes, corner_rows, corner_cols, slot_counts,
    first_weight, first_bias, second_weight, second_bias,
):
    sampled, cells = sample(
        specimen, sampler_noise, probe_field, amplitudes[0, 0],
        corner_rows.reshape(-1), corner_cols.reshape(-1), slot_counts.reshape(-1),
    )
    return subtract_prior(cells, sampled, first_weight, first_bias, second_weight, second_bias)


def solution(mesh):
    return jax.shard_map(
        shards,
        mesh=mesh,
        in_specs=(
            P(None, "tile", "scan"),
            P(None, "tile", "scan"),
            P(),
            P("tile", "scan", None, None, None, None),
            P("tile", "scan", None, None),
            P("tile", "scan", None, None),
            P("tile", "scan", None),
            P(),
            P(),
            P(),
            P(),
        ),
        out_specs=P(None, "tile", "scan"),
        check_vma=False,
    )
```

time: 1210 us -> 173 us (0.14)
  the two profiles are of different devices: /device:TPU:11 before, /device:TPU:35 now
where the time goes in v1:
time: 173 us
  Pallas kernels  164 us (95%)
  local copies, waits for them, and re-layouts  8.44 us (5%)
    pallas_call x1, Pallas kernels, sample(): pl.pallas_call(functools.partial(patch_kernel, order, rows_y, tiles, peer...  113 us
    pallas_call x1, Pallas kernels, subtract_prior(): pl.pallas_call(functools.partial(prior_kernel, tiles, peers), out_shape=j...  51.6 us
    unnamed x25, local copies, waits for them, and re-layouts  8.27 us

profile of v1, /device:TPU:35, one launch (start us, length us, event | category | flops | bytes accessed | tf_op | source)
XLA Modules:
  0.0 172.8 jit_solution(9341884451916935186)
XLA Ops:
  0.0 0.0 copy-start.6
  0.0 0.0 copy-start.7
  0.0 0.0 copy-start.10
  0.0 0.0 copy-start.5
  0.0 0.0 copy-start.9
  0.0 0.8 copy.19
  0.8 0.1 reshape.12.rows_ref
  0.9 0.8 copy.20
  1.7 0.1 reshape.13.cols_ref
  1.8 0.8 copy.21.w1_ref
  2.6 0.0 copy-start
  2.6 1.0 copy-done
  3.6 0.0 copy-start.1
  3.6 1.0 copy-done.1
  4.7 0.0 copy-start.2
  4.7 1.0 copy-done.2
  5.7 0.0 copy-start.3
  5.7 1.0 copy-done.3
  6.8 0.0 copy-start.4
  6.8 1.0 copy-done.4
  7.8 0.0 copy-start.8
  7.8 0.7 copy-done.8
  8.5 112.7 %patches.1 = (f32[2,256,256]{2,1,0:T(8,128)S(1)}, bf16[2,288,512]{2,1,0:T(8,128)(2,1)S(1)}) custom-call(s32[32]{0:T(128)S(1)} %reshape.12.rows_ref, s32[32]{0:T(128)S(1)} %reshape.13.cols_ref, s32[16]{0:T(128)S(1)} %bitcast.7, bf16[16,2,256,256]{3,2,1,0:T(8,128)(2,1)} %bitcast.9, f32[2,256,256]{2,1,0:T(8,128)S(1)} %copy-done, f32[2,256,256]{2,1,0:T(8,128)S(1)} %copy-done.1, ...), custom_call_target="tpu_custom_call" | custom-call | tf_op jit(solution)/shard_map/patches/pallas_call | solution.py:287
  121.2 0.0 copy-done.6
  121.2 0.0 copy-done.7
  121.2 0.0 copy-done.10
  121.2 0.0 copy-done.5
  121.2 0.0 copy-done.9
  121.2 51.6 %prior.1 = f32[2,256,256]{2,1,0:T(8,128)} custom-call(bf16[2,288,512]{2,1,0:T(8,128)(2,1)S(1)} %get-tuple-element.7.cells_ref, f32[2,256,256]{2,1,0:T(8,128)S(1)} %get-tuple-element.8.sampled_ref, bf16[128,18]{1,0:T(8,128)(2,1)S(1)} %copy.21.w1_ref, f32[1,128]{1,0:T(1,128)S(1)} %bitcast.8, bf16[18,128]{1,0:T(8,128)(2,1)S(1)} %copy-done.5, f32[2]{0:T(128)S(1)} %copy-done.10, ...), custom_call_target="tpu_custom_call" | custom-call | tf_op jit(solution)/shard_map/prior/pallas_call | solution.py:384
Async XLA Ops:
  0.0 121.2 %copy-start.6 = (bf16[24,18]{1,0:T(8,128)(2,1)S(1)}, bf16[24,18]{1,0:T(8,128)(2,1)}, u32[]{:S(2)}) copy-start(bf16[24,18]{1,0:T(8,128)(2,1)} %constant.11.clone.sel2_ref) | copy-start | bytes 2596
  0.0 121.2 %copy-start.7 = (bf16[18,24]{1,0:T(8,128)(2,1)S(1)}, bf16[18,24]{1,0:T(8,128)(2,1)}, u32[]{:S(2)}) copy-start(bf16[18,24]{1,0:T(8,128)(2,1)} %constant.10.clone.sel1_ref) | copy-start | bytes 2596
  0.0 121.2 %copy-start.10 = (f32[2]{0:T(128)S(1)}, f32[2]{0:T(128)}, u32[]{:S(2)}) copy-start(f32[2]{0:T(128)} %b2_ref.1) | copy-start | bytes 28
  0.0 121.2 %copy-start.5 = (bf16[18,128]{1,0:T(8,128)(2,1)S(1)}, bf16[18,128]{1,0:T(8,128)(2,1)}, u32[]{:S(2)}) copy-start(bf16[18,128]{1,0:T(8,128)(2,1)} %w2_ref.1) | copy-start | bytes 13828
  0.0 121.2 %copy-start.9 = (f32[128]{0:T(128)S(1)}, f32[128]{0:T(128)}, u32[]{:S(2)}) copy-start(f32[128]{0:T(128)} %param.23) | copy-start | bytes 1540
  2.6 1.0 copy-start
  3.6 1.0 copy-start.1
  4.7 1.0 copy-start.2
  5.7 1.0 copy-start.3
  6.8 1.0 copy-start.4
  7.8 0.7 copy-start.8

commit v2 on v1

--- a/solution.py
+++ b/solution.py
@@ -12,10 +12,10 @@
 NW = 256
 HALF = 128
 EDGE = 16
-WIDE = 384
+PRIOR_ROWS = 264
 CAP = 2
 
-ORDER_16 = [(0, 3), (1, 0), (3, 2), (3, 1), (3, 3), (0, 2), (1, 3), (2, 0), (0, 1), (2, 1), (2, 3), (1, 2), (3, 0), (1, 1), (2, 2)]
+ORDER_16 = [(3, 1), (2, 3), (1, 3), (3, 0), (3, 3), (0, 1), (1, 1), (0, 2), (2, 0), (3, 2), (1, 2), (0, 3), (2, 1), (2, 2), (1, 0)]
 SIDES = [(a, b) for a in (-1, 0, 1) for b in (-1, 0, 1) if (a, b) != (0, 0)]
 
 
@@ -36,7 +36,7 @@
     order, rows_y, tiles, peers,
     rows_ref, cols_ref, counts_ref, amps_ref, spec_ref, noise_ref, probe_ref, fwd_ref, inv_ref,
     out_ref, cells_ref,
-    recv, frame, acc, rim, rim_in, probe2, rolled, wave_in, mid_ref, far_ref,
+    recv, frame, acc, rim, rim_in, probe2, rolled, wave_in, mid_ref, far_ref, wave_ref,
     amp_send, amp_recv, own_sem, halo_send, halo_recv, rim_send, rim_recv, ring_send, ring_recv,
 ):
     f32, bf16 = jnp.float32, jnp.bfloat16
@@ -45,8 +45,10 @@
     rows_z = peers // rows_y
     y, z = s // rows_z, lax.rem(s, rows_z)
 
+    mirror = 1 - 2 * lax.rem(t, 2)
+
     def peer(dy, dz):
-        return lax.rem(y + dy + rows_y, rows_y) * rows_z + lax.rem(z + dz + rows_z, rows_z)
+        return lax.rem(y + mirror * dy + rows_y, rows_y) * rows_z + lax.rem(z + mirror * dz + rows_z, rows_z)
 
     def exists(dt, ds):
         ok_t = {-1: t > 0, 0: t >= 0, 1: t < tiles - 1}[dt]
@@ -91,8 +93,6 @@
         @pl.when(exists(dt, ds))
         def _():
             halo_copy(k, dt, ds).start()
-    for k, (dy, dz) in enumerate(order):
-        amp_copy(k + 1, dy, dz).start()
 
     for part in range(2):
         acc[part] = jnp.zeros((2 * NW, 2 * NW), f32)
@@ -115,19 +115,35 @@
             for part in range(2):
                 frame[part, slice(*at_row), slice(*at_col)] = jnp.zeros((at_row[1] - at_row[0], at_col[1] - at_col[0]), bf16)
 
-    own.wait()
-
-    def step(k, carry):
+    CH = 32
+    lane = lax.broadcasted_iota(jnp.int32, (CH, NW), 1)
+    sub = lax.broadcasted_iota(jnp.int32, (CH, NW), 0)
+
+    def steps_of(k):
         dy, dz = jnp.int32(0), jnp.int32(0)
         for i, (a, b) in enumerate(order):
             dy = jnp.where(k == i + 1, a, dy)
             dz = jnp.where(k == i + 1, b, dz)
+        return dy, dz
+
+    def corners(k):
+        dy, dz = steps_of(k)
         h = peer(-dy, -dz)
-        corner = [(rows_ref[h * CAP + c], cols_ref[h * CAP + c]) for c in range(CAP)]
-        scale = [jnp.where(counts_ref[h] > c, f32(-0.25), f32(0.0)) for c in range(CAP)]
-        CH = 32
-        lane = lax.broadcasted_iota(jnp.int32, (CH, NW), 1)
-        sub = lax.broadcasted_iota(jnp.int32, (CH, NW), 0)
+        return h, [(rows_ref[h * CAP + c], cols_ref[h * CAP + c]) for c in range(CAP)]
+
+    def both(left_ref, right_ref, result):
+        for c in range(CAP):
+            mid = jnp.dot(left_ref[...], wave_in[:, c * NW : (c + 1) * NW], preferred_element_type=f32)
+            for p in range(2):
+                mid_ref[c * NW : (c + 1) * NW, p * NW : (p + 1) * NW] = mid[p * NW : (p + 1) * NW].astype(bf16)
+        for p in range(2):
+            result[:, p * NW : (p + 1) * NW] = jnp.dot(mid_ref[...], right_ref[:, p * NW : (p + 1) * NW], preferred_element_type=f32)
+
+    for k, (dy, dz) in enumerate(order):
+        amp_copy(k + 1, dy, dz).start()
+
+    def outward(k, carry):
+        h, corner = corners(k)
 
         def exits(i, carry):
             base = pl.multiple_of(i * CH, CH)
@@ -141,23 +157,23 @@
                     tile = [[frame[part, pl.ds(base + a * NW, CH), b * NW : (b + 1) * NW].astype(f32) for b in range(2)] for a in range(2)]
                     cell.append(jnp.where(low_row, jnp.where(low_col, tile[1][1], tile[1][0]), jnp.where(low_col, tile[0][1], tile[0][0])))
                     turned = pltpu.roll(jnp.concatenate([probe2[part, half, pl.ds(base + NW - r, CH), :] for half in range(2)], 1), shift, 1)
-                    rolled[c, part, pl.ds(base, CH), :] = turned
+                    rolled[k, c, part, pl.ds(base, CH), :] = turned
                     prb.append(turned)
                 wave_in[pl.ds(base, CH), c * NW : (c + 1) * NW] = (prb[0] * cell[0] - prb[1] * cell[1]).astype(bf16)
                 wave_in[pl.ds(base + NW, CH), c * NW : (c + 1) * NW] = (prb[0] * cell[1] + prb[1] * cell[0]).astype(bf16)
             return carry
 
-        lax.fori_loop(0, NW // CH, exits, 0)
-
-        def both(left_ref, right_ref):
-            for c in range(CAP):
-                mid = jnp.dot(left_ref[...], wave_in[:, c * NW : (c + 1) * NW], preferred_element_type=f32)
-                for p in range(2):
-                    mid_ref[c * NW : (c + 1) * NW, p * NW : (p + 1) * NW] = mid[p * NW : (p + 1) * NW].astype(bf16)
-            for p in range(2):
-                far_ref[:, p * NW : (p + 1) * NW] = jnp.dot(mid_ref[...], right_ref[:, p * NW : (p + 1) * NW], preferred_element_type=f32)
-
-        both(fwd_ref, inv_ref)
+        lax.fori_loop(0, NW // CH, exits, 0, unroll=True)
+        both(fwd_ref, inv_ref, far_ref.at[k])
+        return carry
+
+    lax.fori_loop(0, len(order) + 1, outward, 0, unroll=2)
+    own.wait()
+
+    def inward(k, carry):
+        h, corner = corners(k)
+        dy, dz = steps_of(k)
+        scale = [jnp.where(counts_ref[h] > c, f32(-0.25), f32(0.0)) for c in range(CAP)]
 
         @pl.when(k > 0)
         def _():
@@ -169,25 +185,25 @@
         def correct(i, carry):
             base = pl.multiple_of(i * CH, CH)
             for c in range(CAP):
-                fr = far_ref[pl.ds(base + c * NW, CH), :NW]
-                fi = far_ref[pl.ds(base + c * NW, CH), NW:]
+                fr = far_ref[k, pl.ds(base + c * NW, CH), :NW]
+                fi = far_ref[k, pl.ds(base + c * NW, CH), NW:]
                 amp = recv[k, c, pl.ds(base, CH), :].astype(f32)
                 keep = 1.0 - amp * lax.rsqrt(jnp.maximum(fr * fr + fi * fi, 1.0))
                 wave_in[pl.ds(base, CH), c * NW : (c + 1) * NW] = (fr * keep).astype(bf16)
                 wave_in[pl.ds(base + NW, CH), c * NW : (c + 1) * NW] = (fi * keep).astype(bf16)
             return carry
 
-        lax.fori_loop(0, NW // CH, correct, 0)
-        both(inv_ref, fwd_ref)
+        lax.fori_loop(0, NW // CH, correct, 0, unroll=True)
+        both(inv_ref, fwd_ref, wave_ref)
 
         def gather(i, carry):
             base = pl.multiple_of(i * CH, CH)
             grads = []
             for c in range(CAP):
-                wr = far_ref[pl.ds(base + c * NW, CH), :NW]
-                wi = far_ref[pl.ds(base + c * NW, CH), NW:]
-                pr = rolled[c, 0, pl.ds(base, CH), :] * scale[c]
-                pi = rolled[c, 1, pl.ds(base, CH), :] * scale[c]
+                wr = wave_ref[pl.ds(base + c * NW, CH), :NW]
+                wi = wave_ref[pl.ds(base + c * NW, CH), NW:]
+                pr = rolled[k, c, 0, pl.ds(base, CH), :] * scale[c]
+                pi = rolled[k, c, 1, pl.ds(base, CH), :] * scale[c]
                 grads.append((pr * wr + pi * wi, pr * wi - pi * wr))
             for a in range(2):
                 for b in range(2):
@@ -204,10 +220,10 @@
                         acc[part, pl.ds(base + a * NW, CH), b * NW : (b + 1) * NW] = total
             return carry
 
-        lax.fori_loop(0, NW // CH, gather, 0)
+        lax.fori_loop(0, NW // CH, gather, 0, unroll=True)
         return carry
 
-    lax.fori_loop(0, len(order) + 1, step, 0)
+    lax.fori_loop(0, len(order) + 1, inward, 0, unroll=2)
 
     for part in range(2):
         for lo, hi in ((0, HALF), (HALF + NW, 2 * NW)):
@@ -296,13 +312,14 @@
             pltpu.VMEM((2, 2 * NW, 2 * NW), bf16),
             pltpu.VMEM((2, 2 * NW, 2 * NW), bf16),
             pltpu.VMEM((2, 2, 2 * NW, HALF), f32),
-            pltpu.VMEM((CAP, 2, NW, NW), f32),
+            pltpu.VMEM((peers, CAP, 2, NW, NW), f32),
             pltpu.VMEM((2 * NW, 2 * NW), bf16),
             pltpu.VMEM((2 * NW, 2 * NW), bf16),
+            pltpu.VMEM((peers, 2 * NW, 2 * NW), f32),
             pltpu.VMEM((2 * NW, 2 * NW), f32),
             dma((peers,)), dma((peers,)), dma, dma((8,)), dma((8,)), dma((8,)), dma((8,)), dma((8,)), dma((8,)),
         ],
-        compiler_params=pltpu.CompilerParams(collective_id=0, has_side_effects=True, vmem_limit_bytes=48 << 20),
+        compiler_params=pltpu.CompilerParams(collective_id=0, has_side_effects=True, vmem_limit_bytes=60 << 20),
         name="patches",
     )(rows, cols, counts, amps, specimen, noise, probe, jnp.asarray(forward), jnp.asarray(inverse))
 
@@ -343,34 +360,47 @@
         for k in (6, 7):
             taps[v, pl.ds(k, rows, stride=8), :] = jnp.ones((rows, 128), f32)
 
-    lane = lax.broadcasted_iota(jnp.int32, (24, WIDE), 1)
-    inside = jnp.logical_and(jnp.logical_or(lane > 0, s > 0), jnp.logical_or(lane < NW + 1, s < peers - 1))
-    GROUP = 6
+    GROUP = 44
+    lane = lax.broadcasted_iota(jnp.int32, (24, 128), 1)
+    left_ok = jnp.logical_or(lane > 0, s > 0)
+    extra_ok = jnp.logical_and(lane < 2, jnp.logical_or(lane < 1, s < peers - 1))
 
     def group(g, carry):
         older, old = carry
+        windows, extra = [], None
+        for j in range(GROUP):
+            start = pl.multiple_of((g * GROUP + j + EDGE - 2) * 8, 8)
+            windows += [taps[0, pl.ds(start, 24), :], taps[1, pl.ds(start, 24), :]]
+            last = jnp.where(lane < 2, taps[2, pl.ds(start, 24), :], 0.0)
+            last = pltpu.roll(last, 2 * j, 1) if j else last
+            extra = last if extra is None else extra + last
+        window = jnp.concatenate([v.astype(bf16) for v in windows + [extra]], 1)
+        pre = jnp.dot(first, window, preferred_element_type=f32)
+        hidden = (pre + pre * jnp.tanh(pre)).astype(bf16)
+        mixed_all = jnp.dot(second, hidden, preferred_element_type=f32)
+        tail = mixed_all[:, GROUP * 256 :]
         for j in range(GROUP):
             index = g * GROUP + j
-            start = pl.multiple_of((index + EDGE - 2) * 8, 8)
-            window = jnp.concatenate([taps[v, pl.ds(start, 24), :] for v in range(3)], 1).astype(bf16)
-            pre = jnp.dot(first, window, preferred_element_type=f32)
-            hidden = (pre + pre * jnp.tanh(pre)).astype(bf16)
             here = jnp.logical_and(jnp.logical_or(index > 0, t > 0), jnp.logical_or(index < NW + 1, t < tiles - 1))
-            mixed = jnp.where(jnp.logical_and(inside, here), jnp.dot(second, hidden, preferred_element_type=f32), 0.0)
-            done = older + mixed[16:24]
+            last = pltpu.roll(tail, 128 - 2 * j, 1) if j else tail
+            mixed = [
+                jnp.where(jnp.logical_and(left_ok, here), mixed_all[:, 256 * j : 256 * j + 128], 0.0),
+                jnp.where(here, mixed_all[:, 256 * j + 128 : 256 * j + 256], 0.0),
+                jnp.where(jnp.logical_and(extra_ok, here), last, 0.0),
+            ]
             for v in range(3):
-                mixed_sum[v, pl.ds(pl.multiple_of(index * 8, 8), 8), :] = done[:, v * 128 : (v + 1) * 128]
-            older = old + mixed[8:16]
-            old = mixed[0:8]
+                mixed_sum[v, pl.ds(pl.multiple_of(index * 8, 8), 8), :] = older[v] + mixed[v][16:24]
+            older = [old[v] + mixed[v][8:16] for v in range(3)]
+            old = [mixed[v][0:8] for v in range(3)]
         return older, old
 
-    zero = jnp.zeros((8, WIDE), f32)
-    lax.fori_loop(0, (NW + 2) // GROUP, group, (zero, zero))
+    zero = [jnp.zeros((8, 128), f32)] * 3
+    lax.fori_loop(0, PRIOR_ROWS // GROUP, group, (zero, zero))
     for c in range(2):
         total = None
         for dx in range(3):
             part = jnp.concatenate([mixed_sum[v, pl.ds(16 + 3 * c + dx, NW, stride=8), :] for v in range(3)], 1)
-            part = (pltpu.roll(part, WIDE - dx, 1) if dx else part)[:, :NW]
+            part = (pltpu.roll(part, 384 - dx, 1) if dx else part)[:, :NW]
             total = part if total is None else total + part
         out_ref[c] = sampled_ref[c] - (total + b2_ref[c])
 
@@ -388,7 +418,7 @@
         out_specs=vmem,
         scratch_shapes=[
             pltpu.VMEM((3, 8 * (NW + 2 * EDGE), 128), f32),
-            pltpu.VMEM((3, 8 * (NW + 2), 128), f32),
+            pltpu.VMEM((3, 8 * PRIOR_ROWS, 128), f32),
         ],
         compiler_params=pltpu.CompilerParams(vmem_limit_bytes=32 << 20),
         name="prior",

time: 173 us -> 108 us (0.62)
  the two profiles are of different devices: /device:TPU:35 before, /device:TPU:11 now
where the time goes in v2:
time: 108 us
  Pallas kernels  102 us (94%)
  local copies, waits for them, and re-layouts  5.69 us (5%)
    pallas_call x1, Pallas kernels, sample(): pl.pallas_call(functools.partial(patch_kernel, order, rows_y, tiles, peer...  89.1 us
    pallas_call x1, Pallas kernels, subtract_prior(): pl.pallas_call(functools.partial(prior_kernel, tiles, peers), out_shape=j...  12.7 us
    unnamed x17, local copies, waits for them, and re-layouts  4.49 us

profile of v2, /device:TPU:11, one launch (start us, length us, event | category | flops | bytes accessed | tf_op | source)
XLA Modules:
  0.0 107.5 jit_solution(12506245935740735919)
XLA Ops:
  0.0 0.0 copy-start.3
  0.0 0.0 copy-start.4
  0.0 0.0 copy-start.6
  0.0 0.0 copy-start.2
  0.0 0.0 copy-start.5
  0.0 0.8 copy.19
  0.8 0.6 reshape.12.rows_ref
  1.4 0.8 copy.20
  2.2 0.6 reshape.13.cols_ref
  2.8 0.8 copy.21.w1_ref
  3.6 89.1 %patches.1 = (f32[2,256,256]{2,1,0:T(8,128)}, bf16[2,288,512]{2,1,0:T(8,128)(2,1)}) custom-call(s32[32]{0:T(128)} %reshape.12.rows_ref, s32[32]{0:T(128)} %reshape.13.cols_ref, s32[16]{0:T(128)} %bitcast.9, bf16[16,2,256,256]{3,2,1,0:T(8,128)(2,1)} %bitcast.8, f32[2,256,256]{2,1,0:T(8,128)} %spec_ref.1, f32[2,256,256]{2,1,0:T(8,128)} %noise_ref.1, ...), custom_call_target="tpu_custom_call" | custom-call | tf_op jit(solution)/shard_map/patches/pallas_call | solution.py:303
  92.7 0.0 copy-done.3
  92.7 0.0 copy-done.4
  92.8 0.0 copy-done.6
  92.8 0.0 copy-done.2
  92.8 0.0 copy-done.5
  92.8 0.0 copy-start
  92.8 1.1 copy-done
  93.8 0.0 copy-start.1
  93.9 1.0 copy-done.1
  94.9 12.7 %prior.1 = f32[2,256,256]{2,1,0:T(8,128)} custom-call(bf16[2,288,512]{2,1,0:T(8,128)(2,1)S(1)} %copy-done, f32[2,256,256]{2,1,0:T(8,128)S(1)} %copy-done.1, bf16[128,18]{1,0:T(8,128)(2,1)S(1)} %copy.21.w1_ref, f32[1,128]{1,0:T(1,128)S(1)} %bitcast.7, bf16[18,128]{1,0:T(8,128)(2,1)S(1)} %copy-done.2, f32[2]{0:T(128)S(1)} %copy-done.6, ...), custom_call_target="tpu_custom_call" | custom-call | tf_op jit(solution)/shard_map/prior/pallas_call | solution.py:414
Async XLA Ops:
  0.0 92.7 %copy-start.3 = (bf16[24,18]{1,0:T(8,128)(2,1)S(1)}, bf16[24,18]{1,0:T(8,128)(2,1)}, u32[]{:S(2)}) copy-start(bf16[24,18]{1,0:T(8,128)(2,1)} %constant.11.clone.sel2_ref) | copy-start | bytes 2596
  0.0 92.7 %copy-start.4 = (bf16[18,24]{1,0:T(8,128)(2,1)S(1)}, bf16[18,24]{1,0:T(8,128)(2,1)}, u32[]{:S(2)}) copy-start(bf16[18,24]{1,0:T(8,128)(2,1)} %constant.10.clone.sel1_ref) | copy-start | bytes 2596
  0.0 92.8 %copy-start.6 = (f32[2]{0:T(128)S(1)}, f32[2]{0:T(128)}, u32[]{:S(2)}) copy-start(f32[2]{0:T(128)} %b2_ref.1) | copy-start | bytes 28
  0.0 92.8 %copy-start.2 = (bf16[18,128]{1,0:T(8,128)(2,1)S(1)}, bf16[18,128]{1,0:T(8,128)(2,1)}, u32[]{:S(2)}) copy-start(bf16[18,128]{1,0:T(8,128)(2,1)} %w2_ref.1) | copy-start | bytes 13828
  0.0 92.8 %copy-start.5 = (f32[128]{0:T(128)S(1)}, f32[128]{0:T(128)}, u32[]{:S(2)}) copy-start(f32[128]{0:T(128)} %param.23) | copy-start | bytes 1540
  92.8 1.1 copy-start
  93.8 1.0 copy-start.1

commit v3 on v2

--- a/solution.py
+++ b/solution.py
@@ -15,7 +15,8 @@
 PRIOR_ROWS = 264
 CAP = 2
 
-ORDER_16 = [(3, 1), (2, 3), (1, 3), (3, 0), (3, 3), (0, 1), (1, 1), (0, 2), (2, 0), (3, 2), (1, 2), (0, 3), (2, 1), (2, 2), (1, 0)]
+ORDER_16 = [(3, 1), (1, 3), (2, 3), (1, 1), (3, 0), (2, 0), (3, 3), (1, 2), (0, 1), (0, 3), (2, 1), (3, 2), (1, 0), (0, 2), (2, 2)]
+ISSUE_16 = [0, 2, 1, 4, 6, 8, 3, 13, 5, 11, 7, 9, 10, 14, 12]
 SIDES = [(a, b) for a in (-1, 0, 1) for b in (-1, 0, 1) if (a, b) != (0, 0)]
 
 
@@ -33,7 +34,7 @@
 
 
 def patch_kernel(
-    order, rows_y, tiles, peers,
+    order, issue, rows_y, tiles, peers,
     rows_ref, cols_ref, counts_ref, amps_ref, spec_ref, noise_ref, probe_ref, fwd_ref, inv_ref,
     out_ref, cells_ref,
     recv, frame, acc, rim, rim_in, probe2, rolled, wave_in, mid_ref, far_ref, wave_ref,
@@ -129,7 +130,7 @@
     def corners(k):
         dy, dz = steps_of(k)
         h = peer(-dy, -dz)
-        return h, [(rows_ref[h * CAP + c], cols_ref[h * CAP + c]) for c in range(CAP)]
+        return h, [(rows_ref[c, h], cols_ref[c, h]) for c in range(CAP)]
 
     def both(left_ref, right_ref, result):
         for c in range(CAP):
@@ -139,8 +140,8 @@
         for p in range(2):
             result[:, p * NW : (p + 1) * NW] = jnp.dot(mid_ref[...], right_ref[:, p * NW : (p + 1) * NW], preferred_element_type=f32)
 
-    for k, (dy, dz) in enumerate(order):
-        amp_copy(k + 1, dy, dz).start()
+    for k in issue:
+        amp_copy(k + 1, *order[k]).start()
 
     def outward(k, carry):
         h, corner = corners(k)
@@ -292,16 +293,16 @@
 def sample(specimen, noise, probe, amps, rows, cols, counts):
     tiles, peers = lax.axis_size("tile"), lax.axis_size("scan")
     if peers == 16:
-        order, rows_y = ORDER_16, 4
+        order, issue, rows_y = ORDER_16, ISSUE_16, 4
     else:
-        order, rows_y = [(0, b) for b in range(1, peers)], 1
+        order, issue, rows_y = [(0, b) for b in range(1, peers)], list(range(peers - 1)), 1
     forward, inverse = dft_matrices()
     f32, bf16 = jnp.float32, jnp.bfloat16
     smem = pl.BlockSpec(memory_space=pltpu.SMEM)
     vmem = pl.BlockSpec(memory_space=pltpu.VMEM)
     dma = pltpu.SemaphoreType.DMA
     return pl.pallas_call(
-        functools.partial(patch_kernel, order, rows_y, tiles, peers),
+        functools.partial(patch_kernel, order, issue, rows_y, tiles, peers),
         out_shape=(jax.ShapeDtypeStruct((2, NW, NW), f32), jax.ShapeDtypeStruct((2, NW + 2 * EDGE, 2 * NW), bf16)),
         in_specs=[smem, smem, smem, pl.BlockSpec(memory_space=pl.ANY), vmem, vmem, vmem, vmem, vmem],
         out_specs=(vmem, vmem),
@@ -346,7 +347,7 @@
     bias = jnp.sum(jnp.where(square, b1_ref[...], 0.0), axis=1, keepdims=True) * 0.5
     high = bias.astype(bf16).astype(f32)
     column = lax.broadcasted_iota(jnp.int32, (128, 24), 1)
-    first = jnp.dot(w1_ref[...], sel1_ref[...], preferred_element_type=f32)
+    first = lax.dot_general(w1_ref[...], sel1_ref[...], (((0,), (0,)), ((), ())), preferred_element_type=f32)
     first = (first + jnp.where(column == 6, high, 0.0) + jnp.where(column == 7, bias - high, 0.0)).astype(bf16)
     second = jnp.dot(sel2_ref[...], w2_ref[...], preferred_element_type=f32).astype(bf16)
 
@@ -422,7 +423,7 @@
         ],
         compiler_params=pltpu.CompilerParams(vmem_limit_bytes=32 << 20),
         name="prior",
-    )(cells, sampled, first_weight, first_bias.reshape(1, -1), second_weight, second_bias, jnp.asarray(one), jnp.asarray(two))
+    )(cells, sampled, first_weight.T, first_bias.reshape(1, -1), second_weight, second_bias, jnp.asarray(one), jnp.asarray(two))
 
 
 def shards(
@@ -431,7 +432,7 @@
 ):
     sampled, cells = sample(
         specimen, sampler_noise, probe_field, amplitudes[0, 0],
-        corner_rows.reshape(-1), corner_cols.reshape(-1), slot_counts.reshape(-1),
+        corner_rows[0, 0].T, corner_cols[0, 0].T, slot_counts[0, 0],
     )
     return subtract_prior(cells, sampled, first_weight, first_bias, second_weight, second_bias)
 

time: 108 us -> 101 us (0.935)
  local copies, waits for them, and re-layouts: 5.69 us -> 2.12 us
  Pallas kernels: 102 us -> 98.9 us
    pallas_call x1, Pallas kernels: 89.1 us -> 86.3 us  [sample(): pl.pallas_call(functools.partial(patch_kernel, order, issue, rows_y, tile...]
    unnamed x17 -> x16, local copies, waits for them, and re-layouts: 4.49 us -> 2.12 us
    reshape x2 -> x0, local copies, waits for them, and re-layouts: 1.19 us -> none  [the longest x1 0.6 us: shards(): corner_rows.reshape(-1)]
where the time goes in v3:
time: 101 us
  Pallas kernels  98.9 us (98%)
  local copies, waits for them, and re-layouts  2.12 us (2%)
    pallas_call x1, Pallas kernels, sample(): pl.pallas_call(functools.partial(patch_kernel, order, issue, rows_y, tile...  86.3 us
    pallas_call x1, Pallas kernels, subtract_prior(): pl.pallas_call(functools.partial(prior_kernel, tiles, peers), out_shape=j...  12.6 us
    unnamed x16, local copies, waits for them, and re-layouts  2.12 us

profile of v3, /device:TPU:11, one launch (start us, length us, event | category | flops | bytes accessed | tf_op | source)
XLA Modules:
  0.0 101.1 jit_solution(7101406077492548979)
XLA Ops:
  0.0 0.0 copy-start.4
  0.0 0.0 copy-start.5
  0.0 0.0 copy-start.7
  0.0 0.0 copy-start.3
  0.0 0.0 copy-start.6
  0.0 0.0 copy-start.2
  0.0 86.3 %patches.1 = (f32[2,256,256]{2,1,0:T(8,128)}, bf16[2,288,512]{2,1,0:T(8,128)(2,1)}) custom-call(s32[2,16]{1,0:T(2,128)} %bitcast.13, s32[2,16]{1,0:T(2,128)} %bitcast.14, s32[16]{0:T(128)} %bitcast.15, bf16[16,2,256,256]{3,2,1,0:T(8,128)(2,1)} %bitcast.12, f32[2,256,256]{2,1,0:T(8,128)} %spec_ref.1, f32[2,256,256]{2,1,0:T(8,128)} %noise_ref.1, ...), custom_call_target="tpu_custom_call" | custom-call | tf_op jit(solution)/shard_map/patches/pallas_call | solution.py:304
  86.3 0.0 copy-done.4
  86.4 0.0 copy-done.5
  86.4 0.0 copy-done.7
  86.4 0.0 copy-done.3
  86.4 0.0 copy-done.6
  86.4 0.0 copy-done.2
  86.4 0.0 copy-start
  86.4 1.1 %copy-done = bf16[2,288,512]{2,1,0:T(8,128)(2,1)S(1)} copy-done((bf16[2,288,512]{2,1,0:T(8,128)(2,1)S(1)}, bf16[2,288,512]{2,1,0:T(8,128)(2,1)}, u32[]{:S(2)}) %copy-start) | copy-done | bytes 589848
  87.5 0.0 copy-start.1
  87.5 1.0 %copy-done.1 = f32[2,256,256]{2,1,0:T(8,128)S(1)} copy-done((f32[2,256,256]{2,1,0:T(8,128)S(1)}, f32[2,256,256]{2,1,0:T(8,128)}, u32[]{:S(2)}) %copy-start.1) | copy-done | bytes 524312
  88.5 12.6 %prior.1 = f32[2,256,256]{2,1,0:T(8,128)} custom-call(bf16[2,288,512]{2,1,0:T(8,128)(2,1)S(1)} %copy-done, f32[2,256,256]{2,1,0:T(8,128)S(1)} %copy-done.1, bf16[18,128]{1,0:T(8,128)(2,1)S(1)} %bitcast.10, f32[1,128]{1,0:T(1,128)S(1)} %bitcast.11, bf16[18,128]{1,0:T(8,128)(2,1)S(1)} %copy-done.3, f32[2]{0:T(128)S(1)} %copy-done.7, ...), custom_call_target="tpu_custom_call" | custom-call | tf_op jit(solution)/shard_map/prior/pallas_call | solution.py:415
Async XLA Ops:
  0.0 86.4 %copy-start.4 = (bf16[24,18]{1,0:T(8,128)(2,1)S(1)}, bf16[24,18]{1,0:T(8,128)(2,1)}, u32[]{:S(2)}) copy-start(bf16[24,18]{1,0:T(8,128)(2,1)} %constant.11.clone.sel2_ref) | copy-start | bytes 2596
  0.0 86.4 %copy-start.5 = (bf16[18,24]{1,0:T(8,128)(2,1)S(1)}, bf16[18,24]{1,0:T(8,128)(2,1)}, u32[]{:S(2)}) copy-start(bf16[18,24]{1,0:T(8,128)(2,1)} %constant.10.clone.sel1_ref) | copy-start | bytes 2596
  0.0 86.4 %copy-start.7 = (f32[2]{0:T(128)S(1)}, f32[2]{0:T(128)}, u32[]{:S(2)}) copy-start(f32[2]{0:T(128)} %b2_ref.1) | copy-start | bytes 28
  0.0 86.4 %copy-start.3 = (bf16[18,128]{1,0:T(8,128)(2,1)S(1)}, bf16[18,128]{1,0:T(8,128)(2,1)}, u32[]{:S(2)}) copy-start(bf16[18,128]{1,0:T(8,128)(2,1)} %w2_ref.1) | copy-start | bytes 13828
  0.0 86.4 %copy-start.6 = (f32[128]{0:T(128)S(1)}, f32[128]{0:T(128)}, u32[]{:S(2)}) copy-start(f32[128]{0:T(128)} %param.23) | copy-start | bytes 1540
  0.0 86.4 %copy-start.2 = (bf16[128,18]{0,1:T(8,128)(2,1)S(1)}, bf16[128,18]{0,1:T(8,128)(2,1)}, u32[]{:S(2)}) copy-start(bf16[128,18]{0,1:T(8,128)(2,1)} %param.22) | copy-start | bytes 13828
  86.4 1.1 %copy-start = (bf16[2,288,512]{2,1,0:T(8,128)(2,1)S(1)}, bf16[2,288,512]{2,1,0:T(8,128)(2,1)}, u32[]{:S(2)}) copy-start(bf16[2,288,512]{2,1,0:T(8,128)(2,1)} %get-tuple-element.7.cells_ref) | copy-start | bytes 1769476
  87.5 1.0 %copy-start.1 = (f32[2,256,256]{2,1,0:T(8,128)S(1)}, f32[2,256,256]{2,1,0:T(8,128)}, u32[]{:S(2)}) copy-start(f32[2,256,256]{2,1,0:T(8,128)} %get-tuple-element.8.sampled_ref) | copy-start | bytes 1572868

commit v4 on v3

--- a/solution.py
+++ b/solution.py
@@ -12,6 +12,7 @@
 NW = 256
 HALF = 128
 EDGE = 16
+GROUP = 24
 PRIOR_ROWS = 264
 CAP = 2
 
@@ -36,7 +37,9 @@
 def patch_kernel(
     order, issue, rows_y, tiles, peers,
     rows_ref, cols_ref, counts_ref, amps_ref, spec_ref, noise_ref, probe_ref, fwd_ref, inv_ref,
-    out_ref, cells_ref,
+    w1_ref, b1_ref, w2_ref, b2_ref, sel1_ref, sel2_ref,
+    out_ref,
+    cells_ref, taps, mixed_sum, first_ref, first_edge, second_ref, second_edge,
     recv, frame, acc, rim, rim_in, probe2, rolled, wave_in, mid_ref, far_ref, wave_ref,
     amp_send, amp_recv, own_sem, halo_send, halo_recv, rim_send, rim_recv, ring_send, ring_recv,
 ):
@@ -115,6 +118,25 @@
             at_row, at_col = span(dt, (384, 512), (128, 384), (0, 128)), span(ds, (384, 512), (128, 384), (0, 128))
             for part in range(2):
                 frame[part, slice(*at_row), slice(*at_col)] = jnp.zeros((at_row[1] - at_row[0], at_col[1] - at_col[0]), bf16)
+
+    square = lax.broadcasted_iota(jnp.int32, (128, 128), 0) == lax.broadcasted_iota(jnp.int32, (128, 128), 1)
+    bias = jnp.sum(jnp.where(square, b1_ref[...], 0.0), axis=1, keepdims=True) * 0.5
+    high = bias.astype(bf16).astype(f32)
+    for v in range(3):
+        column = lax.broadcasted_iota(jnp.int32, (128, 32), 1)
+        at = 24 if v else 6
+        weights = lax.dot_general(w1_ref[...], sel1_ref[v], (((0,), (0,)), ((), ())), preferred_element_type=f32)
+        weights = (weights + jnp.where(column == at, high, 0.0) + jnp.where(column == at + 1, bias - high, 0.0)).astype(bf16)
+        if v == 0:
+            first_ref[...] = weights
+        else:
+            first_edge[(v - 1) * 128 : v * 128, :] = weights
+    second_ref[...] = jnp.dot(sel2_ref[0], w2_ref[...], preferred_element_type=f32).astype(bf16)
+    for side in range(2):
+        for v in range(2):
+            second_edge[side, :, v * 128 : (v + 1) * 128] = jnp.dot(
+                sel2_ref[1 + 2 * side + v], w2_ref[...], preferred_element_type=f32
+            ).astype(bf16)
 
     CH = 32
     lane = lax.broadcasted_iota(jnp.int32, (CH, NW), 1)
@@ -267,6 +289,45 @@
         @pl.when(exists(dt, ds))
         def _():
             ring_copy(k, dt, ds).start()
+    def moved(rows256, dx):
+        return rows256 if dx == 1 else pltpu.roll(rows256, 1 if dx == 0 else NW - 1, 1)
+
+    for part in range(2):
+        for dx in range(3):
+            shifted = moved(out_ref[part], dx)
+            for v in range(2):
+                taps[v, pl.ds(16 + 3 * part + dx, NW, stride=8), :] = shifted[:, v * 128 : (v + 1) * 128]
+    for v in range(2):
+        for k in (6, 7):
+            taps[v, pl.ds(k, NW + 4, stride=8), :] = jnp.ones((NW + 4, 128), f32)
+
+    mlane = lax.broadcasted_iota(jnp.int32, (24, 128), 1)
+    inner = (mlane > 0, mlane < 127)
+
+    def hidden_of(weights, window):
+        pre = jnp.dot(weights, window, preferred_element_type=f32)
+        return pre + pre * jnp.tanh(pre)
+
+    def mixed_rows(starts):
+        window = jnp.concatenate([taps[v, pl.ds(start, 24), :].astype(bf16) for start in starts for v in range(2)], 1)
+        return jnp.dot(second_ref[...], hidden_of(first_ref[:, :24], window).astype(bf16), preferred_element_type=f32)
+
+    def group(g, carry):
+        older, old = carry
+        mixed_all = mixed_rows([pl.multiple_of((g * GROUP + j) * 8, 8) for j in range(GROUP)])
+        for j in range(GROUP):
+            index = g * GROUP + j
+            here = jnp.logical_and(index > 1, index < NW)
+            mixed = [jnp.where(jnp.logical_and(inner[v], here), mixed_all[:, (2 * j + v) * 128 : (2 * j + v + 1) * 128], 0.0) for v in range(2)]
+            for v in range(2):
+                mixed_sum[v, pl.ds(pl.multiple_of(index * 8, 8), 8), :] = older[v] + mixed[v][16:24]
+            older = [old[v] + mixed[v][8:16] for v in range(2)]
+            old = [mixed[v][0:8] for v in range(2)]
+        return older, old
+
+    zero = [jnp.zeros((8, 128), f32)] * 2
+    lax.fori_loop(0, PRIOR_ROWS // GROUP, group, (zero, zero))
+
     for k, (dt, ds) in enumerate(SIDES):
         here = exists(-dt, -ds)
 
@@ -280,6 +341,64 @@
             for part in range(2):
                 cells_ref[part, slice(*at_row), slice(*at_col)] = jnp.zeros((at_row[1] - at_row[0], at_col[1] - at_col[0]), bf16)
 
+    for part in range(2):
+        for at, first_row, take in ((0, 0, 14), (NW + 2, EDGE + NW, 0)):
+            strip = cells_ref[part, first_row : first_row + EDGE, HALF : HALF + NW].astype(f32)
+            for dx in range(3):
+                shifted = moved(strip, dx)
+                for v in range(2):
+                    for i in range(2):
+                        taps[v, (at + i) * 8 + 3 * part + dx : (at + i) * 8 + 3 * part + dx + 1, :] = shifted[take + i : take + i + 1, v * 128 : (v + 1) * 128]
+    border = (0, 1, NW, NW + 1)
+    mixed_all = mixed_rows([8 * index for index in border])
+    for j, index in enumerate(border):
+        here = {0: t > 0, NW + 1: t < tiles - 1}.get(index, t >= 0)
+        for v in range(2):
+            mixed = jnp.where(jnp.logical_and(inner[v], here), mixed_all[:, (2 * j + v) * 128 : (2 * j + v + 1) * 128], 0.0)
+            for dy in range(3):
+                row = index + 2 - dy
+                if 2 <= row < NW + 2:
+                    mixed_sum[v, row * 8 : row * 8 + 8, :] += mixed[8 * dy : 8 * dy + 8]
+
+    WIDE = 384
+    strip_lane = lax.broadcasted_iota(jnp.int32, (NW + 2 * EDGE, 128), 1)
+    row_lane = lax.broadcasted_iota(jnp.int32, (8, WIDE), 1)
+    constant = jnp.where(lax.broadcasted_iota(jnp.int32, (8, WIDE), 0) < 2, 1.0, 0.0)
+    edge_sum = None
+    for side in range(2):
+        planes = [cells_ref[part, :, side * NW : (side + 1) * NW].astype(f32) for part in range(2)]
+        strips = [pltpu.roll(planes[part], NW - 126 + 4 * part, 1)[:, :128] for part in range(2)]
+        strip = jnp.where(strip_lane < 4, strips[0], strips[1])
+        strip = jnp.concatenate([strip, jnp.zeros((WIDE - NW - 2 * EDGE, 128), f32)], 0).T[:8]
+        window = jnp.concatenate([pltpu.roll(strip, 1, 1), strip, pltpu.roll(strip, WIDE - 1, 1), constant], 0).astype(bf16)
+        hidden = hidden_of(first_edge[...], window)
+        outer = lax.broadcasted_iota(jnp.int32, (NW, WIDE), 0) < 128 if side == 0 else lax.broadcasted_iota(jnp.int32, (NW, WIDE), 0) >= 128
+        gone = s == 0 if side == 0 else s == peers - 1
+        hidden = jnp.where(jnp.logical_and(outer, gone), 0.0, hidden).astype(bf16)
+        mixed = jnp.dot(second_edge[side], hidden, preferred_element_type=f32)
+        edge_sum = mixed if edge_sum is None else edge_sum + mixed
+    by_dy = []
+    for dy in range(3):
+        piece = edge_sum[8 * dy : 8 * dy + 8]
+        piece = jnp.where(jnp.logical_and(row_lane == EDGE - 1, t == 0), 0.0, piece)
+        piece = jnp.where(jnp.logical_and(row_lane == EDGE + NW, t == tiles - 1), 0.0, piece)
+        by_dy.append(piece if dy == 1 else pltpu.roll(piece, 1 if dy == 0 else WIDE - 1, 1))
+    columns = by_dy[0] + by_dy[1] + by_dy[2]
+    columns = jnp.concatenate([columns, jnp.zeros((120, WIDE), f32)], 0).T[EDGE : EDGE + NW]
+    out_lane = lax.broadcasted_iota(jnp.int32, (NW, 128), 1)
+    for part in range(2):
+        halves = [jnp.zeros((NW, 128), f32), jnp.zeros((NW, 128), f32)]
+        for dx in range(3):
+            sums = jnp.concatenate([mixed_sum[v, pl.ds(16 + 3 * part + dx, NW, stride=8), :] for v in range(2)], 1)
+            sums = sums if dx == 1 else pltpu.roll(sums, 1 if dx == 0 else NW - 1, 1)
+            halves = [halves[v] + sums[:, v * 128 : (v + 1) * 128] for v in range(2)]
+        left = pltpu.roll(columns, (128 - 2 * part) % 128, 1) if part else columns
+        right = pltpu.roll(columns, 126 - 4 - 2 * part, 1)
+        halves[0] = halves[0] + jnp.where(out_lane < 2, left, 0.0)
+        halves[1] = halves[1] + jnp.where(out_lane >= 126, right, 0.0)
+        for v in range(2):
+            at = slice(v * 128, (v + 1) * 128)
+            out_ref[part, :, at] = out_ref[part, :, at] - (halves[v] + b2_ref[part])
     for k, (dt, ds) in enumerate(SIDES):
         @pl.when(exists(dt, ds))
         def _():
@@ -290,23 +409,31 @@
         amp_copy(k + 1, dy, dz).wait_send()
 
 
-def sample(specimen, noise, probe, amps, rows, cols, counts):
+def sample(specimen, noise, probe, amps, rows, cols, counts, w1, b1, w2, b2):
     tiles, peers = lax.axis_size("tile"), lax.axis_size("scan")
     if peers == 16:
         order, issue, rows_y = ORDER_16, ISSUE_16, 4
     else:
         order, issue, rows_y = [(0, b) for b in range(1, peers)], list(range(peers - 1)), 1
     forward, inverse = dft_matrices()
+    one, two = tap_selectors()
     f32, bf16 = jnp.float32, jnp.bfloat16
     smem = pl.BlockSpec(memory_space=pltpu.SMEM)
     vmem = pl.BlockSpec(memory_space=pltpu.VMEM)
     dma = pltpu.SemaphoreType.DMA
     return pl.pallas_call(
         functools.partial(patch_kernel, order, issue, rows_y, tiles, peers),
-        out_shape=(jax.ShapeDtypeStruct((2, NW, NW), f32), jax.ShapeDtypeStruct((2, NW + 2 * EDGE, 2 * NW), bf16)),
-        in_specs=[smem, smem, smem, pl.BlockSpec(memory_space=pl.ANY), vmem, vmem, vmem, vmem, vmem],
-        out_specs=(vmem, vmem),
+        out_shape=jax.ShapeDtypeStruct((2, NW, NW), f32),
+        in_specs=[smem, smem, smem, pl.BlockSpec(memory_space=pl.ANY)] + [vmem] * 5 + [vmem, vmem, vmem, smem, vmem, vmem],
+        out_specs=vmem,
         scratch_shapes=[
+            pltpu.VMEM((2, NW + 2 * EDGE, 2 * NW), bf16),
+            pltpu.VMEM((2, 8 * (PRIOR_ROWS + 2), 128), f32),
+            pltpu.VMEM((2, 8 * PRIOR_ROWS, 128), f32),
+            pltpu.VMEM((128, 32), bf16),
+            pltpu.VMEM((NW, 32), bf16),
+            pltpu.VMEM((24, 128), bf16),
+            pltpu.VMEM((2, 24, NW), bf16),
             pltpu.VMEM((peers, CAP, NW, NW), bf16),
             pltpu.VMEM((2, 2 * NW, 2 * NW), bf16),
             pltpu.VMEM((2, 2 * NW, 2 * NW), f32),
@@ -321,120 +448,36 @@
             dma((peers,)), dma((peers,)), dma, dma((8,)), dma((8,)), dma((8,)), dma((8,)), dma((8,)), dma((8,)),
         ],
         compiler_params=pltpu.CompilerParams(collective_id=0, has_side_effects=True, vmem_limit_bytes=60 << 20),
-        name="patches",
-    )(rows, cols, counts, amps, specimen, noise, probe, jnp.asarray(forward), jnp.asarray(inverse))
+        name="step",
+    )(rows, cols, counts, amps, specimen, noise, probe, jnp.asarray(forward), jnp.asarray(inverse),
+      w1, b1, w2, b2, jnp.asarray(one), jnp.asarray(two))
 
 
 def tap_selectors():
-    first = np.zeros((18, 24), np.float32)
-    second = np.zeros((24, 18), np.float32)
+    first = np.zeros((3, 18, 32), np.float32)
+    second = np.zeros((5, 24, 18), np.float32)
     for c in range(2):
         for dy in range(3):
             for dx in range(3):
-                first[9 * c + 3 * dy + dx, 8 * dy + 3 * c + dx] = 0.5
-                second[8 * dy + 3 * c + dx, 9 * c + 3 * dy + dx] = 1.0
+                tap = 9 * c + 3 * dy + dx
+                first[0, tap, 8 * dy + 3 * c + dx] = 0.5
+                first[1, tap, 8 * dy + 4 * c + dx] = 0.5
+                first[2, tap, 8 * dy + 4 * c + dx + 1] = 0.5
+                second[0, 8 * dy + 3 * c + dx, tap] = 1.0
+            for side, half, dx, at in ((0, 0, 0, 0), (0, 1, 1, 0), (0, 1, 0, 1), (1, 0, 2, 0), (1, 0, 1, 1), (1, 1, 2, 1)):
+                second[1 + 2 * side + half, 8 * dy + 4 * side + 2 * c + at, 9 * c + 3 * dy + dx] = 1.0
     return first.astype(jnp.bfloat16), second.astype(jnp.bfloat16)
-
-
-def prior_kernel(
-    tiles, peers, cells_ref, sampled_ref, w1_ref, b1_ref, w2_ref, b2_ref, sel1_ref, sel2_ref, out_ref, taps, mixed_sum,
-):
-    f32, bf16 = jnp.float32, jnp.bfloat16
-    t = lax.axis_index("tile")
-    s = lax.axis_index("scan")
-    rows = NW + 2 * EDGE
-    square = lax.broadcasted_iota(jnp.int32, (128, 128), 0) == lax.broadcasted_iota(jnp.int32, (128, 128), 1)
-    bias = jnp.sum(jnp.where(square, b1_ref[...], 0.0), axis=1, keepdims=True) * 0.5
-    high = bias.astype(bf16).astype(f32)
-    column = lax.broadcasted_iota(jnp.int32, (128, 24), 1)
-    first = lax.dot_general(w1_ref[...], sel1_ref[...], (((0,), (0,)), ((), ())), preferred_element_type=f32)
-    first = (first + jnp.where(column == 6, high, 0.0) + jnp.where(column == 7, bias - high, 0.0)).astype(bf16)
-    second = jnp.dot(sel2_ref[...], w2_ref[...], preferred_element_type=f32).astype(bf16)
-
-    for c in range(2):
-        plane = cells_ref[c].astype(f32)
-        for dx in range(3):
-            moved = pltpu.roll(plane, 2 * NW - (126 + dx), 1)
-            for v in range(3):
-                taps[v, pl.ds(3 * c + dx, rows, stride=8), :] = moved[:, v * 128 : (v + 1) * 128]
-    for v in range(3):
-        for k in (6, 7):
-            taps[v, pl.ds(k, rows, stride=8), :] = jnp.ones((rows, 128), f32)
-
-    GROUP = 44
-    lane = lax.broadcasted_iota(jnp.int32, (24, 128), 1)
-    left_ok = jnp.logical_or(lane > 0, s > 0)
-    extra_ok = jnp.logical_and(lane < 2, jnp.logical_or(lane < 1, s < peers - 1))
-
-    def group(g, carry):
-        older, old = carry
-        windows, extra = [], None
-        for j in range(GROUP):
-            start = pl.multiple_of((g * GROUP + j + EDGE - 2) * 8, 8)
-            windows += [taps[0, pl.ds(start, 24), :], taps[1, pl.ds(start, 24), :]]
-            last = jnp.where(lane < 2, taps[2, pl.ds(start, 24), :], 0.0)
-            last = pltpu.roll(last, 2 * j, 1) if j else last
-            extra = last if extra is None else extra + last
-        window = jnp.concatenate([v.astype(bf16) for v in windows + [extra]], 1)
-        pre = jnp.dot(first, window, preferred_element_type=f32)
-        hidden = (pre + pre * jnp.tanh(pre)).astype(bf16)
-        mixed_all = jnp.dot(second, hidden, preferred_element_type=f32)
-        tail = mixed_all[:, GROUP * 256 :]
-        for j in range(GROUP):
-            index = g * GROUP + j
-            here = jnp.logical_and(jnp.logical_or(index > 0, t > 0), jnp.logical_or(index < NW + 1, t < tiles - 1))
-            last = pltpu.roll(tail, 128 - 2 * j, 1) if j else tail
-            mixed = [
-                jnp.where(jnp.logical_and(left_ok, here), mixed_all[:, 256 * j : 256 * j + 128], 0.0),
-                jnp.where(here, mixed_all[:, 256 * j + 128 : 256 * j + 256], 0.0),
-                jnp.where(jnp.logical_and(extra_ok, here), last, 0.0),
-            ]
-            for v in range(3):
-                mixed_sum[v, pl.ds(pl.multiple_of(index * 8, 8), 8), :] = older[v] + mixed[v][16:24]
-            older = [old[v] + mixed[v][8:16] for v in range(3)]
-            old = [mixed[v][0:8] for v in range(3)]
-        return older, old
-
-    zero = [jnp.zeros((8, 128), f32)] * 3
-    lax.fori_loop(0, PRIOR_ROWS // GROUP, group, (zero, zero))
-    for c in range(2):
-        total = None
-        for dx in range(3):
-            part = jnp.concatenate([mixed_sum[v, pl.ds(16 + 3 * c + dx, NW, stride=8), :] for v in range(3)], 1)
-            part = (pltpu.roll(part, 384 - dx, 1) if dx else part)[:, :NW]
-            total = part if total is None else total + part
-        out_ref[c] = sampled_ref[c] - (total + b2_ref[c])
-
-
-def subtract_prior(cells, sampled, first_weight, first_bias, second_weight, second_bias):
-    tiles, peers = lax.axis_size("tile"), lax.axis_size("scan")
-    f32 = jnp.float32
-    smem = pl.BlockSpec(memory_space=pltpu.SMEM)
-    vmem = pl.BlockSpec(memory_space=pltpu.VMEM)
-    one, two = tap_selectors()
-    return pl.pallas_call(
-        functools.partial(prior_kernel, tiles, peers),
-        out_shape=jax.ShapeDtypeStruct((2, NW, NW), f32),
-        in_specs=[vmem, vmem, vmem, vmem, vmem, smem, vmem, vmem],
-        out_specs=vmem,
-        scratch_shapes=[
-            pltpu.VMEM((3, 8 * (NW + 2 * EDGE), 128), f32),
-            pltpu.VMEM((3, 8 * PRIOR_ROWS, 128), f32),
-        ],
-        compiler_params=pltpu.CompilerParams(vmem_limit_bytes=32 << 20),
-        name="prior",
-    )(cells, sampled, first_weight.T, first_bias.reshape(1, -1), second_weight, second_bias, jnp.asarray(one), jnp.asarray(two))
 
 
 def shards(
     specimen, sampler_noise, probe_field, amplitudes, corner_rows, corner_cols, slot_counts,
     first_weight, first_bias, second_weight, second_bias,
 ):
-    sampled, cells = sample(
+    return sample(
         specimen, sampler_noise, probe_field, amplitudes[0, 0],
         corner_rows[0, 0].T, corner_cols[0, 0].T, slot_counts[0, 0],
+        first_weight.T, first_bias.reshape(1, -1), second_weight, second_bias,
     )
-    return subtract_prior(cells, sampled, first_weight, first_bias, second_weight, second_bias)
 
 
 def solution(mesh):

time: 101 us -> 91.8 us (0.909); the launches traced: 101 us -> 90.4 us
  Pallas kernels: 98.9 us -> 88.5 us
    pallas_call x1 -> x0, Pallas kernels: 12.6 us -> none  [subtract_prior(): pl.pallas_call(functools.partial(prior_kernel, tiles, peers), out_shape=j...]
    pallas_call x1, Pallas kernels: 86.3 us -> 88.5 us  [sample(): pl.pallas_call(functools.partial(patch_kernel, order, issue, rows_y, tile...]
    unnamed x16 -> x1, local copies, waits for them, and re-layouts: 2.12 us -> 1.87 us
where the time goes in v4:
time: 91.8 us; the launch traced here: 90.4 us
  Pallas kernels  88.5 us (96%)
  local copies, waits for them, and re-layouts  1.87 us (2%)
    pallas_call x1, Pallas kernels, sample(): pl.pallas_call(functools.partial(patch_kernel, order, issue, rows_y, tile...  88.5 us
    unnamed x1, local copies, waits for them, and re-layouts  1.87 us

profile of v4, /device:TPU:11, one launch (start us, length us, event | category | flops | bytes accessed | tf_op | source)
XLA Modules:
  0.0 90.4 jit_solution(10337860695327046457)
XLA Ops:
  0.0 88.5 %step.1 = f32[2,256,256]{2,1,0:T(8,128)} custom-call(s32[2,16]{1,0:T(2,128)} %bitcast.12, s32[2,16]{1,0:T(2,128)} %bitcast.13, s32[16]{0:T(128)} %bitcast.14, bf16[16,2,256,256]{3,2,1,0:T(8,128)(2,1)} %bitcast.10, f32[2,256,256]{2,1,0:T(8,128)} %spec_ref.1, f32[2,256,256]{2,1,0:T(8,128)} %noise_ref.1, f32[2,256,256]{2,1,0:T(8,128)} %probe_ref.1, ...), custom_call_target="tpu_custom_call" | custom-call | tf_op jit(solution)/shard_map/step/pallas_call | solution.py:424
  88.5 1.9 %copy.17 = f32[2,256,256]{2,1,0:T(8,128)} copy(f32[2,256,256]{2,1,0:T(8,128)} %step.1) | data formatting | bytes 1048576

commit v5 on v4

--- a/solution.py
+++ b/solution.py
@@ -36,9 +36,10 @@
 
 def patch_kernel(
     order, issue, rows_y, tiles, peers,
-    rows_ref, cols_ref, counts_ref, amps_ref, spec_ref, noise_ref, probe_ref, fwd_ref, inv_ref,
+    rows_ref, cols_ref, counts_ref, amps_ref, spec_hbm, noise_hbm, probe_hbm, fwd_hbm, inv_hbm,
     w1_ref, b1_ref, w2_ref, b2_ref, sel1_ref, sel2_ref,
     out_ref,
+    spec_ref, noise_ref, probe_ref, fwd_ref, inv_ref, load_sem,
     cells_ref, taps, mixed_sum, first_ref, first_edge, second_ref, second_edge,
     recv, frame, acc, rim, rim_in, probe2, rolled, wave_in, mid_ref, far_ref, wave_ref,
     amp_send, amp_recv, own_sem, halo_send, halo_recv, rim_send, rim_recv, ring_send, ring_recv,
@@ -72,8 +73,17 @@
             def _():
                 pl.semaphore_signal(barrier, inc=1, device_id=(t + dt, s + ds), device_id_type=MESH)
 
+    loads = [
+        pltpu.make_async_copy(source, place, load_sem.at[i])
+        for i, (source, place) in enumerate(
+            ((spec_hbm, spec_ref), (noise_hbm, noise_ref), (probe_hbm, probe_ref), (fwd_hbm, fwd_ref), (inv_hbm, inv_ref))
+        )
+    ]
+    for load in loads:
+        load.start()
     own = pltpu.make_async_copy(amps_ref.at[s], recv.at[0], own_sem)
     own.start()
+    loads[0].wait()
     for part in range(2):
         frame[part, HALF : HALF + NW, HALF : HALF + NW] = spec_ref[part].astype(bf16)
     pl.semaphore_wait(barrier, expected)
@@ -86,6 +96,14 @@
             device_id=(t + dt, s + ds), device_id_type=MESH,
         )
 
+    def relay_copy(k, dt, ds):
+        columns = span(ds, slice(384, 512), None, slice(0, 128))
+        return pltpu.make_async_remote_copy(
+            src_ref=frame.at[:, span(dt, slice(128, 256), None, slice(256, 384)), columns],
+            dst_ref=frame.at[:, span(dt, slice(384, 512), None, slice(0, 128)), columns],
+            send_sem=halo_send.at[k], recv_sem=halo_recv.at[k], device_id=(t + dt, s), device_id_type=MESH,
+        )
+
     def amp_copy(k, dy, dz):
         d = peer(dy, dz)
         return pltpu.make_async_remote_copy(
@@ -93,11 +111,15 @@
             device_id=(t, d), device_id_type=MESH,
         )
 
-    for k, (dt, ds) in enumerate(SIDES):
+    straight = [(k, dt, ds) for k, (dt, ds) in enumerate(SIDES) if dt * ds == 0]
+    diagonal = [(k, dt, ds) for k, (dt, ds) in enumerate(SIDES) if dt * ds != 0]
+    for k, dt, ds in straight:
         @pl.when(exists(dt, ds))
         def _():
             halo_copy(k, dt, ds).start()
 
+    for load in loads[1:]:
+        load.wait()
     for part in range(2):
         acc[part] = jnp.zeros((2 * NW, 2 * NW), f32)
         acc[part, HALF : HALF + NW, HALF : HALF + NW] = spec_ref[part] + 0.5 * noise_ref[part]
@@ -106,18 +128,29 @@
             probe2[part, half, :NW, :] = columns
             probe2[part, half, NW:, :] = columns
 
-    for k, (dt, ds) in enumerate(SIDES):
+    def take_halo(k, dt, ds, copy):
         here = exists(-dt, -ds)
 
         @pl.when(here)
         def _():
-            halo_copy(k, dt, ds).wait_recv()
+            copy(k, dt, ds).wait_recv()
 
         @pl.when(jnp.logical_not(here))
         def _():
             at_row, at_col = span(dt, (384, 512), (128, 384), (0, 128)), span(ds, (384, 512), (128, 384), (0, 128))
             for part in range(2):
                 frame[part, slice(*at_row), slice(*at_col)] = jnp.zeros((at_row[1] - at_row[0], at_col[1] - at_col[0]), bf16)
+
+    for k, dt, ds in straight:
+        take_halo(k, dt, ds, halo_copy)
+    for k, dt, ds in diagonal:
+        @pl.when(jnp.logical_and(exists(dt, 0), exists(0, -ds)))
+        def _():
+            relay_copy(k, dt, ds).start()
+    for k in issue:
+        amp_copy(k + 1, *order[k]).start()
+    for k, dt, ds in diagonal:
+        take_halo(k, dt, ds, relay_copy)
 
     square = lax.broadcasted_iota(jnp.int32, (128, 128), 0) == lax.broadcasted_iota(jnp.int32, (128, 128), 1)
     bias = jnp.sum(jnp.where(square, b1_ref[...], 0.0), axis=1, keepdims=True) * 0.5
@@ -162,8 +195,6 @@
         for p in range(2):
             result[:, p * NW : (p + 1) * NW] = jnp.dot(mid_ref[...], right_ref[:, p * NW : (p + 1) * NW], preferred_element_type=f32)
 
-    for k in issue:
-        amp_copy(k + 1, *order[k]).start()
 
     def outward(k, carry):
         h, corner = corners(k)
@@ -403,8 +434,15 @@
         @pl.when(exists(dt, ds))
         def _():
             ring_copy(k, dt, ds).wait_send()
+            rim_copy(k, dt, ds).wait_send()
+    for k, dt, ds in straight:
+        @pl.when(exists(dt, ds))
+        def _():
             halo_copy(k, dt, ds).wait_send()
-            rim_copy(k, dt, ds).wait_send()
+    for k, dt, ds in diagonal:
+        @pl.when(jnp.logical_and(exists(dt, 0), exists(0, -ds)))
+        def _():
+            relay_copy(k, dt, ds).wait_send()
     for k, (dy, dz) in enumerate(order):
         amp_copy(k + 1, dy, dz).wait_send()
 
@@ -423,10 +461,16 @@
     dma = pltpu.SemaphoreType.DMA
     return pl.pallas_call(
         functools.partial(patch_kernel, order, issue, rows_y, tiles, peers),
-        out_shape=jax.ShapeDtypeStruct((2, NW, NW), f32),
-        in_specs=[smem, smem, smem, pl.BlockSpec(memory_space=pl.ANY)] + [vmem] * 5 + [vmem, vmem, vmem, smem, vmem, vmem],
+        out_shape=pltpu.VMEM((2, NW, NW), f32),
+        in_specs=[smem, smem, smem, pl.BlockSpec(memory_space=pl.ANY)] + [pl.BlockSpec(memory_space=pl.ANY)] * 5 + [vmem, vmem, vmem, smem, vmem, vmem],
         out_specs=vmem,
         scratch_shapes=[
+            pltpu.VMEM((2, NW, NW), f32),
+            pltpu.VMEM((2, NW, NW), f32),
+            pltpu.VMEM((2, NW, NW), f32),
+            pltpu.VMEM((2 * NW, 2 * NW), bf16),
+            pltpu.VMEM((2 * NW, 2 * NW), bf16),
+            dma((5,)),
             pltpu.VMEM((2, NW + 2 * EDGE, 2 * NW), bf16),
             pltpu.VMEM((2, 8 * (PRIOR_ROWS + 2), 128), f32),
             pltpu.VMEM((2, 8 * PRIOR_ROWS, 128), f32),

time: 91.8 us -> 84.5 us (0.920)
  Pallas kernels: 88.5 us -> 83.1 us
  local copies, waits for them, and re-layouts: 1.87 us -> 0.8 us
    pallas_call x1, Pallas kernels: 88.5 us -> 83.1 us  [sample(): pl.pallas_call(functools.partial(patch_kernel, order, issue, rows_y, tile...]
    unnamed x1, local copies, waits for them, and re-layouts: 1.87 us -> 0.8 us
where the time goes in v5:
time: 84.5 us; the launch traced here: 83.9 us
  Pallas kernels  83.1 us (98%)
    pallas_call x1, Pallas kernels, sample(): pl.pallas_call(functools.partial(patch_kernel, order, issue, rows_y, tile...  83.1 us

profile of v5, /device:TPU:11, one launch (start us, length us, event | category | flops | bytes accessed | tf_op | source)
XLA Modules:
  0.0 83.9 jit_solution(14594146974226903328)
XLA Ops:
  0.0 83.1 %step.1 = f32[2,256,256]{2,1,0:T(8,128)S(1)} custom-call(s32[2,16]{1,0:T(2,128)} %bitcast.12, s32[2,16]{1,0:T(2,128)} %bitcast.13, s32[16]{0:T(128)} %bitcast.14, bf16[16,2,256,256]{3,2,1,0:T(8,128)(2,1)} %bitcast.10, f32[2,256,256]{2,1,0:T(8,128)} %spec_hbm.1, f32[2,256,256]{2,1,0:T(8,128)} %noise_hbm.1, f32[2,256,256]{2,1,0:T(8,128)} %probe_hbm.1, ...), custom_call_target="tpu_custom_call" | custom-call | tf_op jit(solution)/shard_map/step/pallas_call | solution.py:462
  83.1 0.8 copy.17

commit v6 on v5

--- a/solution.py
+++ b/solution.py
@@ -12,7 +12,7 @@
 NW = 256
 HALF = 128
 EDGE = 16
-GROUP = 24
+GROUP = 44
 PRIOR_ROWS = 264
 CAP = 2
 
@@ -491,7 +491,7 @@
             pltpu.VMEM((2 * NW, 2 * NW), f32),
             dma((peers,)), dma((peers,)), dma, dma((8,)), dma((8,)), dma((8,)), dma((8,)), dma((8,)), dma((8,)),
         ],
-        compiler_params=pltpu.CompilerParams(collective_id=0, has_side_effects=True, vmem_limit_bytes=60 << 20),
+        compiler_params=pltpu.CompilerParams(collective_id=0, has_side_effects=True, vmem_limit_bytes=62 << 20),
         name="step",
     )(rows, cols, counts, amps, specimen, noise, probe, jnp.asarray(forward), jnp.asarray(inverse),
       w1, b1, w2, b2, jnp.asarray(one), jnp.asarray(two))

time: 84.5 us -> 83.8 us (level)
  no operation moved by 1% of the time
where the time goes in v6:
time: 83.8 us; the launch traced here: 83.2 us
  Pallas kernels  82.4 us (98%)
    pallas_call x1, Pallas kernels, sample(): pl.pallas_call(functools.partial(patch_kernel, order, issue, rows_y, tile...  82.4 us

profile of v6, /device:TPU:11, one launch (start us, length us, event | category | flops | bytes accessed | tf_op | source)
XLA Modules:
  0.0 83.2 jit_solution(8278136903691233785)
XLA Ops:
  0.0 82.4 %step.1 = f32[2,256,256]{2,1,0:T(8,128)S(1)} custom-call(s32[2,16]{1,0:T(2,128)} %bitcast.12, s32[2,16]{1,0:T(2,128)} %bitcast.13, s32[16]{0:T(128)} %bitcast.14, bf16[16,2,256,256]{3,2,1,0:T(8,128)(2,1)} %bitcast.10, f32[2,256,256]{2,1,0:T(8,128)} %spec_hbm.1, f32[2,256,256]{2,1,0:T(8,128)} %noise_hbm.1, f32[2,256,256]{2,1,0:T(8,128)} %probe_hbm.1, ...), custom_call_target="tpu_custom_call" | custom-call | tf_op jit(solution)/shard_map/step/pallas_call | solution.py:462
  82.4 0.8 copy.17

commit v7 on v6

--- a/solution.py
+++ b/solution.py
@@ -281,8 +281,7 @@
 
     for part in range(2):
         for lo, hi in ((0, HALF), (HALF + NW, 2 * NW)):
-            rim[part, lo:hi, :] = acc[part, lo:hi, :].astype(bf16)
-            rim[part, HALF : HALF + NW, lo:hi] = acc[part, HALF : HALF + NW, lo:hi].astype(bf16)
+            rim[part, :, lo:hi] = acc[part, :, lo:hi].astype(bf16)
 
     def rim_copy(k, dt, ds):
         where = (slice(None), slice(*span(dt, (0, 128), (128, 384), (384, 512))), slice(*span(ds, (0, 128), (128, 384), (384, 512))))
@@ -291,13 +290,21 @@
             device_id=(t + dt, s + ds), device_id_type=MESH,
         )
 
-    for k, (dt, ds) in enumerate(SIDES):
+    for k, dt, ds in [side for side in straight if side[2] != 0] + diagonal:
         @pl.when(exists(dt, ds))
         def _():
             rim_copy(k, dt, ds).start()
     for part in range(2):
+        for lo, hi in ((0, HALF), (HALF + NW, 2 * NW)):
+            rim[part, lo:hi, HALF : HALF + NW] = acc[part, lo:hi, HALF : HALF + NW].astype(bf16)
+    for k, dt, ds in straight:
+        if ds == 0:
+            @pl.when(exists(dt, ds))
+            def _():
+                rim_copy(k, dt, ds).start()
+    for part in range(2):
         out_ref[part] = acc[part, HALF : HALF + NW, HALF : HALF + NW]
-    for k, (dt, ds) in enumerate(SIDES):
+    for k, dt, ds in sorted(straight, key=lambda side: side[2] != 0) + diagonal:
         @pl.when(exists(-dt, -ds))
         def _():
             rim_copy(k, dt, ds).wait_recv()

time: 83.8 us -> 83.3 us (level); the launches traced: 83.2 us -> 81.8 us
  Pallas kernels: 82.4 us -> 81 us
    pallas_call x1, Pallas kernels: 82.4 us -> 81 us  [sample(): pl.pallas_call(functools.partial(patch_kernel, order, issue, rows_y, tile...]
where the time goes in v7:
time: 83.3 us; the launch traced here: 81.8 us
  Pallas kernels  81 us (97%)
    pallas_call x1, Pallas kernels, sample(): pl.pallas_call(functools.partial(patch_kernel, order, issue, rows_y, tile...  81 us

profile of v7, /device:TPU:11, one launch (start us, length us, event | category | flops | bytes accessed | tf_op | source)
XLA Modules:
  0.0 81.8 jit_solution(16655174321946429508)
XLA Ops:
  0.0 81.0 %step.1 = f32[2,256,256]{2,1,0:T(8,128)S(1)} custom-call(s32[2,16]{1,0:T(2,128)} %bitcast.12, s32[2,16]{1,0:T(2,128)} %bitcast.13, s32[16]{0:T(128)} %bitcast.14, bf16[16,2,256,256]{3,2,1,0:T(8,128)(2,1)} %bitcast.10, f32[2,256,256]{2,1,0:T(8,128)} %spec_hbm.1, f32[2,256,256]{2,1,0:T(8,128)} %noise_hbm.1, f32[2,256,256]{2,1,0:T(8,128)} %probe_hbm.1, ...), custom_call_target="tpu_custom_call" | custom-call | tf_op jit(solution)/shard_map/step/pallas_call | solution.py:469
  81.0 0.8 copy.17

commit v8 on v7

--- a/solution.py
+++ b/solution.py
@@ -323,7 +323,7 @@
             device_id=(t + dt, s + ds), device_id_type=MESH,
         )
 
-    for k, (dt, ds) in enumerate(SIDES):
+    for k, dt, ds in sorted(straight, key=lambda side: side[2] == 0) + diagonal:
         @pl.when(exists(dt, ds))
         def _():
             ring_copy(k, dt, ds).start()

time: 83.3 us -> 83.3 us (level)
  no operation moved by 1% of the time
where the time goes in v8:
time: 83.3 us; the launch traced here: 81.8 us
  Pallas kernels  81 us (97%)
    pallas_call x1, Pallas kernels, sample(): pl.pallas_call(functools.partial(patch_kernel, order, issue, rows_y, tile...  81 us

profile of v8, /device:TPU:11, one launch (start us, length us, event | category | flops | bytes accessed | tf_op | source)
XLA Modules:
  0.0 81.8 jit_solution(17649931656911225466)
XLA Ops:
  0.0 81.0 %step.1 = f32[2,256,256]{2,1,0:T(8,128)S(1)} custom-call(s32[2,16]{1,0:T(2,128)} %bitcast.12, s32[2,16]{1,0:T(2,128)} %bitcast.13, s32[16]{0:T(128)} %bitcast.14, bf16[16,2,256,256]{3,2,1,0:T(8,128)(2,1)} %bitcast.10, f32[2,256,256]{2,1,0:T(8,128)} %spec_hbm.1, f32[2,256,256]{2,1,0:T(8,128)} %noise_hbm.1, f32[2,256,256]{2,1,0:T(8,128)} %probe_hbm.1, ...), custom_call_target="tpu_custom_call" | custom-call | tf_op jit(solution)/shard_map/step/pallas_call | solution.py:469
  81.0 0.8 copy.17
